TPU v7x, 32 devices: a whole 2x2x4 slice. The times are simulated.
32 devices in a mesh: section: 4 (over y, x), dp: 8 (over z, core).
Axes of the slice: x: 2, y: 2, z: 4, core: 2. Of those that a mesh axis runs over, the one named last changes fastest.
Arguments:
- boundary: bfloat16 [4, 8192, 768], P('section', 'dp'), may hold values from -6 to 6
- bucket_ids: int32 [2, 16, 4], P(None, 'dp'), may hold values from 0 to 3, as said below
- w_in: bfloat16 [2, 768, 3072], P(None, 'dp'), may hold values from -0.21875 to 0.21875
- b_in: float32 [2, 3072], replicated, may hold values from -3 to 3
- w_out: bfloat16 [2, 3072, 768], P(None, 'dp'), may hold values from -0.109375 to 0.109375
- b_out: float32 [2, 768], replicated, may hold values from -3 to 3
- gain_one: float32 [2, 768], replicated, may hold values from 0.5 to 1.5
- shift_one: float32 [2, 768], replicated, may hold values from -3 to 3
- gain_two: float32 [2, 768], replicated, may hold values from 0.5 to 1.5
- shift_two: float32 [2, 768], replicated, may hold values from -3 to 3
Outputs:
- result: float32 [4, 8192, 768], P('section', 'dp')
- grad_w_in: float32 [2, 768, 3072], P(None, 'dp')
- grad_b_in: float32 [2, 3072], P(None, 'dp')
- grad_w_out: float32 [2, 3072, 768], P(None, 'dp')
- grad_b_out: float32 [2, 768], P(None, 'dp')
- grad_gain_one: float32 [2, 768], P(None, 'dp')
- grad_shift_one: float32 [2, 768], P(None, 'dp')
- grad_gain_two: float32 [2, 768], P(None, 'dp')
- grad_shift_two: float32 [2, 768], P(None, 'dp')
Inputs may be any that keep to these rules, and one draw needn't show every extreme that they name: `bucket_ids`: each row lists the buckets of the sequences packed into one block of 512 tokens in order; bucket k holds sequences of 128 * 2**k tokens, 3 marks an empty slot; the used slots come first and their lengths add up to 512 exactly.
All inputs are finite; a program needn't handle non-finite values.
Results may differ from a plain program's by a relative error of at most 0.014.
Values may be sent and summed in bfloat16 or wider, within the bound.
No kernel may reach another device: no remote copies, remote signals or barrier semaphores. Data moves between devices by JAX's collectives and lax.ppermute only.
A program may use at most 256 MiB of HBM per device.

v0:
```python
from functools import partial
import math

import jax
import jax.numpy as jnp
import numpy as np
from jax import lax
from jax.experimental import pallas as pl
from jax.experimental.pallas import tpu as pltpu
from jax.sharding import PartitionSpec as P

AXES = ("section", "dp")
F32 = jnp.float32
BF16 = jnp.bfloat16
BLOCKS = 4
FORWARD_COST, BACKWARD_COST = 10**10, 10**10
ROW_STEP = 256

VMEM = pl.BlockSpec(memory_space=pltpu.VMEM)
SMEM = pl.BlockSpec(memory_space=pltpu.SMEM)
HBM = pl.BlockSpec(memory_space=pltpu.HBM)
LATE, EARLY = "late", "early"


class Place:
    def __init__(self):
        self.n_section = lax.axis_size("section")
        self.n_dp = lax.axis_size("dp")
        self.chips = self.n_dp // 2
        self.section = lax.axis_index("section")
        self.dp = lax.axis_index("dp")
        self.core = self.dp % 2

    def permute(self, value, target):
        pairs = []
        for section in range(self.n_section):
            for chip in range(self.chips):
                for core in range(2):
                    to_section, to_chip, to_core = target(section, chip, core)
                    source = section * self.n_dp + chip * 2 + core
                    pairs.append((source, to_section * self.n_dp + to_chip * 2 + to_core))
        return lax.ppermute(value, AXES, pairs)

    def swap_core(self, value):
        return self.permute(value, lambda s, z, c: (s, z, 1 - c))

    def swap_layer(self, value):
        return self.permute(value, lambda s, z, c: (s ^ 1, z, c))

    def plane_one(self, value):
        return self.permute(value, lambda s, z, c: (s ^ (1 + c), z, c))

    def plane_two(self, value):
        return self.permute(value, lambda s, z, c: (s ^ (2 - c), z, c))

    def along_z(self, value, flip):
        return self.permute(value, lambda s, z, c: (s, z ^ flip, c))


class Spot:
    def __init__(self, by_permutes=True):
        dp = lax.axis_index("dp")
        self.core = dp % 2
        if by_permutes:
            self.section, self.chip = lax.axis_index("section"), dp // 2
            self.chips = lax.axis_size("dp") // 2
            self.held = (1 + self.core, 3, 2 - self.core, 0)
        else:
            self.section, self.held = 0, (0, 1, 2, 3)

    def block(self, turn):
        return self.section ^ self.held[turn]

    def turn_of(self, block):
        flip = block ^ self.section
        side = jnp.where(flip == self.held[0], 0, 2)
        return jnp.where(flip == 3, 1, jnp.where(flip == 0, 3, side))


def dft_tables(length):
    positions = np.arange(length)
    angles = (positions[:, None] * positions[None, :] % length) * (2.0 * math.pi) / length
    scaling = 1.0 / math.sqrt(length)
    return (np.cos(angles) * scaling, np.sin(angles) * scaling)


def sequence_tiles(base_len):
    cos_tiles, sin_tiles = [], []
    for parts in (1, 2, 4):
        cos_table, sin_table = dft_tables(parts * base_len)
        for i in range(parts):
            for j in range(parts):
                window = (
                    slice(i * base_len, (i + 1) * base_len),
                    slice(j * base_len, (j + 1) * base_len),
                )
                cos_tiles.append(cos_table[window])
                sin_tiles.append(sin_table[window])
    cos_tiles.append(np.zeros((base_len, base_len)))
    sin_tiles.append(np.zeros((base_len, base_len)))
    return np.stack(cos_tiles).astype(BF16), np.stack(sin_tiles).astype(BF16)


def tile_numbers(bucket_row, slots):
    parts = jnp.where(bucket_row < 3, 1 << jnp.minimum(bucket_row, 2), 0)
    ends = jnp.cumsum(parts)
    where = jnp.arange(slots, dtype=jnp.int32)
    segment = jnp.sum((where[:, None] >= ends[None, :]).astype(jnp.int32), axis=1)
    one_hot = (segment[:, None] == jnp.arange(slots)[None, :]).astype(jnp.int32)
    start = jnp.sum(one_hot * (ends - parts)[None, :], axis=1)
    size = jnp.sum(one_hot * parts[None, :], axis=1)
    first = jnp.where(size == 1, 0, jnp.where(size == 2, 1, 5))
    place = where - start
    numbers = first[:, None] + place[:, None] * size[:, None] + place[None, :]
    return jnp.where(segment[:, None] == segment[None, :], numbers, 21)


def rows_at(start, size):
    return pl.ds(pl.multiple_of(start, size), size)


def dot(left, right, dims=((1,), (0,))):
    return lax.dot_general(left, right, (dims, ((), ())), preferred_element_type=F32)


def row_steps(count, step=ROW_STEP):
    step = step if count % step == 0 else count

    def run(function):
        for i in range(count // step):
            function(pl.ds(i * step, step))

    return run


def column_sum(values):
    return jnp.sum(values, axis=0, keepdims=True)


class Copies:
    def __init__(self, sems):
        self.sems, self.count = sems, 0

    def start(self, source, target):
        copy = pltpu.make_async_copy(source, target, self.sems.at[self.count])
        copy.start()
        self.count += 1
        return copy


class Late:
    def __init__(self, ref):
        self.buffer = ref

    def __call__(self, parts=None):
        return self.buffer


class Early:
    def __init__(self, ref):
        self.buffer, self.leaving = ref, []

    def push(self, part=None):
        pass


def tie(value, *others):
    return lax.optimization_barrier((value,) + others)[0]


class Order:
    token = None
    cost = FORWARD_COST

    @classmethod
    def begin(cls):
        cls.token = jnp.zeros((8, 128), F32)
        cls.cost = FORWARD_COST

    @classmethod
    def wait(cls, *arrays):
        cls.token = tie(cls.token, *arrays)

    @classmethod
    def mark(cls, *arrays):
        cls.wait(*arrays)
        call(lambda *refs: None, [], [], [], "mark")
        return cls.token


def call(kernel, ins, outs, scratch, name, aliases=None, spare=4 * 2**20):
    buffers = []
    n_ins, n_outs, n_scratch = len(ins), len(outs), len(scratch)
    counts = []

    def run(*refs):
        given, made = list(refs[:n_ins]), list(refs[n_ins + 1 :][:n_outs])
        token_out, refs = refs[n_ins + 1 + n_outs], refs[n_ins + 2 + n_outs :]
        own, held, copies = refs[:n_scratch], list(refs[n_scratch:-1]), Copies(refs[-1])
        late = []
        for i, entry in enumerate(ins):
            if entry[0] is LATE:
                given[i] = Late(given[i])
                late.append(given[i])
        early = []
        for i, out in enumerate(outs):
            if out[0] is EARLY:
                made[i] = Early(made[i])
                early.append(made[i])
        leaving = kernel(*given, *made, *own, copies) or []
        token_out[...] = jnp.zeros_like(token_out)
        for value in late:
            value()
        for copy in leaving + [copy for out in early for copy in out.leaving]:
            copy.wait()
        counts.append(copies.count)

    def spec_of(spec):
        return VMEM if spec in (LATE, EARLY) else spec

    held = list(scratch) + [(a[1].shape, a[1].dtype) for a in ins if a[0] in (LATE, VMEM)]
    held += [out[1:] for out in outs if out[0] in (EARLY, VMEM)]
    needed = sum(math.prod(shape) * jnp.dtype(dtype).itemsize for shape, dtype in held)

    def build(sems):
        return pl.pallas_call(
            run,
            in_specs=[spec_of(entry[0]) for entry in ins] + [HBM],
            out_specs=tuple(spec_of(out[0]) for out in outs) + (VMEM,),
            out_shape=tuple(jax.ShapeDtypeStruct(*out[1:]) for out in outs)
            + (jax.ShapeDtypeStruct((8, 128), F32),),
            scratch_shapes=[pltpu.VMEM(*s) for s in scratch]
            + buffers
            + [pltpu.SemaphoreType.DMA((sems,))],
            compiler_params=pltpu.CompilerParams(vmem_limit_bytes=needed + spare),
            cost_estimate=pl.CostEstimate(flops=Order.cost, bytes_accessed=1000, transcendentals=0),
            input_output_aliases=aliases or {},
            name=name,
        )

    arrays = [entry[1] for entry in ins] + [Order.token]
    jax.eval_shape(build(96), *arrays)
    *made, Order.token = build(max(counts[-1], 1))(*arrays)
    return made


def move(name, terms, unit, outs, targets, extra=None):
    jobs = [
        ([(array, indices[i]) for array, indices in terms], unit, target)
        for i, target in enumerate(targets)
    ]
    if extra is not None:
        jobs.append(extra)
    given = []
    for job_terms, _, _ in jobs:
        for array, _ in job_terms:
            if not any(array is other for other in given):
                given.append(array)

    def run(*refs):
        ins, made = refs[: len(given)], refs[len(given) : len(given) + len(outs)]

        def at(index):
            index = index(Spot()) if callable(index) else index
            return index if index else Ellipsis

        for job_terms, _, (number, target) in jobs:
            parts = [
                next(ref for ref, other in zip(ins, given) if other is array)[at(index)]
                for array, index in job_terms
            ]
            if len(parts) > 1:
                parts = [sum((part.astype(F32) for part in parts[1:]), parts[0].astype(F32))]
            made[number][at(target)] = parts[0].astype(BF16)

    return call(
        run,
        [(VMEM, array) for array in given],
        [(VMEM, shape, BF16) for shape in outs],
        [],
        name,
    )


def pack(name, entries):
    entries = [entry if isinstance(entry, tuple) else (entry, None, None) for entry in entries]
    unit = entries[0][0].shape[-2:]
    sizes = [
        count or (1 if len(array.shape) == 2 else array.shape[0]) for array, _, count in entries
    ]
    starts = [sum(sizes[:i]) for i in range(len(sizes))]

    def run(*refs):
        out = refs[len(entries)]
        for i, (ref, (_, start, count)) in enumerate(zip(refs, entries)):
            source = ref[...] if start is None else ref[pl.ds(start, count)]
            out[pl.ds(starts[i], sizes[i])] = source.reshape((sizes[i],) + unit)

    whole = ((sum(sizes),) + unit, entries[0][0].dtype)
    (packed,) = call(
        run, [(VMEM, entry[0]) for entry in entries], [(VMEM,) + whole], [], name
    )
    return packed


def choose(copies, first, second, buffer):
    is_first = lax.axis_index("section") % 2 == 0
    sem = copies.sems.at[copies.count]
    copies.count += 1
    pair = [pltpu.make_async_copy(source, buffer, sem) for source in (first, second)]
    pl.when(is_first)(pair[0].start)
    pl.when(jnp.logical_not(is_first))(pair[1].start)
    return pair[0]


def prepare_kernel(layers, by_permutes, boundary, w_in, w_out, given, *refs):
    outs, (slab, rows, pieces, copies) = refs[: -4], refs[-4:]
    count = slab.shape[0]
    first, second = (boundary.at[0, pl.ds(i * count, count)] for i in range(2))
    slab_copy = choose(copies, second, first, slab)
    leaving = []
    if by_permutes:
        other_rows, *out_pieces = outs
        spot = Spot()
        width = w_in.shape[2] // (2 * BLOCKS)
        arriving = []
        for block in range(BLOCKS):
            source = w_in.at[:, :, rows_at((2 * block + 1 - spot.core) * width, width)]
            arriving.append(copies.start(source, rows.at[:, :, pl.ds(block * width, width)]))
        high = w_out.shape[1] // BLOCKS
        for layer in range(layers):
            source = w_out.at[layer, rows_at(spot.section * high, high)]
            arriving.append(copies.start(source, pieces.at[layer]))
        for copy in arriving[:BLOCKS]:
            copy.wait()
        leaving.append(copies.start(rows, other_rows))
        for layer in range(layers):
            arriving[BLOCKS + layer].wait()
            leaving.append(copies.start(pieces.at[layer], out_pieces[layer]))
    slab_copy.wait()
    leaving.append(copies.start(slab, given))
    return leaving


class Gather:
    def __init__(self, place, name, w, other_rows, layer, by_rows):
        self.place, self.name, self.by_rows = place, name, by_rows
        self.w, self.other_rows, self.layer = w, other_rows, layer

    def join(self, halves, out_piece=None):
        layer, rows, width = self.layer, self.w.shape[1], self.w.shape[2] // (2 * BLOCKS)
        beside = out_piece is not None
        shape = (2, rows, 2 * width) if beside else (2 * rows, width)

        def run(w, other, *refs):
            out_ref, (out, held, copies) = refs[:-3], refs[-3:]
            spot = Spot()
            own = w.at[layer, :, rows_at((2 * spot.section + spot.core) * width, width)]
            other = other.at[layer, :, rows_at(spot.section * width, width)]
            arriving = []
            for source, core in ((own, spot.core), (other, 1 - spot.core)):
                target = held.at[rows_at(core * rows, rows)]
                if beside:
                    target = held.at[0, :, rows_at(core * width, width)]
                arriving.append(copies.start(source, target))
            if beside:
                arriving.append(copies.start(out_ref[0], held.at[1]))
            for copy in arriving:
                copy.wait()
            return [copies.start(held, out)]

        (piece,) = call(
            run,
            [(HBM, self.w), (HBM, halves)] + ([(HBM, out_piece)] if beside else []),
            [(HBM, shape, BF16)],
            [(shape, BF16)],
            "piece_" + self.name,
        )
        return piece

    def shift(self, piece):
        self.moved = [self.place.along_z(piece, flip) for flip in (1, 2, 3)]

    def one(self):
        self.along = pack("along_" + self.name, self.moved)
        self.from_one = self.place.plane_one(self.along)
        self.from_two = self.place.plane_two(self.along)

    def two(self, *others):
        self.far = self.place.plane_two(tie(self.from_one, *others))

    def sources(self):
        moved = [self.along, self.from_one, self.from_two, self.far]
        return [self.w] + moved if self.by_rows else [self.w, self.other_rows] + moved


def pairs(own, moved):
    _, rows, width = own.shape

    def run(own, moved, pair_in, pair_out, copies):
        for i, ref in enumerate((own, moved)):
            for core in range(2):
                half = pl.ds(core * (width // 2), width // 2)
                pair_in[i, pl.ds(core * rows, rows)] = ref[0, :, half]
            pair_out[i] = ref[1]

    shapes = [((2, 2 * rows, width // 2), BF16), ((2, rows, width), BF16)]
    return call(run, [(VMEM, own), (VMEM, moved)], [(VMEM,) + s for s in shapes], [], "pairs")


def load_in(layer, sources, scratch, copies):
    if len(sources) == 1:
        width = scratch.shape[2]
        return [[copies.start(sources[0].at[:, pl.ds(i * width, width)], scratch.at[i])] for i in range(2)]
    own, other, along, one, two, far = sources
    spot = Spot()
    rows, width = own.shape[1], along.shape[2]
    pairs = []
    for pair in range(2):
        started = []
        for side in range(2):
            turn = 2 * pair + side
            columns = pl.ds(side * width, width)
            block = spot.block(turn)
            source = (one, far, two, along)[turn]
            for apart in range(1, spot.chips):
                chip = spot.chip ^ apart
                target = scratch.at[pair, rows_at(chip * 2 * rows, 2 * rows), columns]
                started.append(copies.start(source.at[apart - 1], target))
            for core, ref, index in (
                (spot.core, own, rows_at((2 * block + spot.core) * width, width)),
                (1 - spot.core, other, rows_at(block * width, width)),
            ):
                target = scratch.at[pair, rows_at((2 * spot.chip + core) * rows, rows), columns]
                started.append(copies.start(ref.at[layer, :, index], target))
        pairs.append(started)
    return pairs


def load_out(layer, sources, scratch, copies):
    if len(sources) == 1:
        return [copies.start(sources[0], scratch)]
    own, along, one, two, far = sources
    spot = Spot()
    shard, rows = own.shape[1], along.shape[1]
    started = []
    for apart in range(spot.chips):
        chip = spot.chip ^ apart
        start = spot.turn_of(chip) * shard
        if apart == 0:
            started.append(copies.start(own.at[layer], scratch.at[rows_at(start, shard), :]))
            continue
        for turn, source in enumerate((one, far, two, along)):
            part = pl.ds(pl.multiple_of(start + spot.block(turn) * rows, rows), rows)
            started.append(copies.start(source.at[apart - 1], scratch.at[part, :]))
    return started


class Scatter:
    def __init__(self, place, name, first, rest, by_rows):
        self.place, self.name, self.rest, self.by_rows = place, name, rest, by_rows
        self.chips, self.unit = rest.shape[1], rest.shape[2:]
        self.from_one = place.plane_one(first)
        self.small = None

    def move(self, stage, terms, sent):
        rows, width = self.unit
        extra, height = None, sent * rows
        if self.small is not None:
            self.small_rows = self.small[0][1].size
            terms_small = [(array, (at,)) for array, at in self.small]
            target = (0, (pl.ds(height, self.small_rows),))
            extra = (terms_small, (self.small_rows, width), target)
            height += self.small_rows
        targets = [(0, (pl.ds(i * rows, rows),)) for i in range(sent)]
        name = stage + "_" + self.name
        (made,) = move(name, terms, self.unit, [(height, width)], targets, extra)
        return made

    def heard(self, sent, received, count):
        if self.small is not None:
            at = pl.ds(count * self.unit[0], self.small_rows)
            self.small = [(sent, at), (received, at)]

    def part(self, i):
        return (pl.ds(i * self.unit[0], self.unit[0]),)

    def two(self):
        terms = [
            (self.rest, [(0, i) for i in range(self.chips)]),
            (self.from_one, [(1, i) for i in range(self.chips)]),
        ]
        second = self.move("two", terms, self.chips)
        self.from_two = self.place.plane_two(second)
        self.heard(second, self.from_two, self.chips)
        return second

    def own_terms(self, aparts):
        return [
            (self.rest, [(1, i) for i in aparts]),
            (self.from_one, [(0, i) for i in aparts]),
            (self.from_two, [self.part(i) for i in aparts]),
        ]

    def three(self):
        pair = self.move("three", self.own_terms([2, 3]), 2)
        self.from_pair = self.place.along_z(pair, 2)
        self.heard(pair, self.from_pair, 2)
        return pair

    def neighbour(self):
        terms = self.own_terms([1]) + [(self.from_pair, [self.part(1)])]
        piece = self.move("next", terms, 1)
        self.from_next = self.place.along_z(piece, 1)
        self.heard(piece, self.from_next, 1)
        return piece

    def four(self):
        if self.by_rows:
            terms = self.own_terms([0]) + [
                (self.from_pair, [self.part(0)]),
                (self.from_next, [self.part(0)]),
            ]
            (self.sum,) = move(
                "four_" + self.name, terms, self.unit, [self.unit], [(0, ())]
            )
            return self.sum
        rows, width = self.unit[0] // 2, self.unit[1]
        parts = [
            lambda spot: (rows_at(spot.core * rows, rows),),
            lambda spot: (rows_at((1 - spot.core) * rows, rows),),
        ]

        def of(head):
            return [lambda spot, part=part: head + part(spot) for part in parts]

        terms = [
            (self.rest, of((1, 0))),
            (self.from_one, of((0, 0))),
            (self.from_two, of(())),
            (self.from_pair, of(())),
            (self.from_next, of(())),
        ]
        targets, extra, height = [(0, ()), (1, (pl.ds(0, rows),))], None, rows
        if self.small is not None:
            height += self.small_rows
            terms_small = [(array, (at,)) for array, at in self.small]
            extra = (terms_small, (self.small_rows, width), (1, (pl.ds(rows, self.small_rows),)))
        self.kept, self.given = move(
            "four_" + self.name, terms, (rows, width), [(rows, width), (height, width)], targets, extra
        )
        self.from_core = self.place.swap_core(self.given)
        return self.kept


def join(name, scatters):
    given = []
    for scatter in scatters:
        given += [scatter.sum] if scatter.by_rows else [scatter.kept, scatter.from_core]
    rows, width = scatters[0].kept.shape
    half, width = width, 2 * width
    with_small = [scatter for scatter in scatters if scatter.small is not None]
    given += [scatter.given for scatter in with_small]
    small_rows = with_small[0].small_rows // 2 if with_small else 0
    count = len(scatters)

    def run(*refs):
        ins, out = list(refs[: len(given)]), refs[len(given)]
        spot = Spot()

        def small(ref, at):
            for i in range(2):
                part = ref[pl.ds(rows + i * small_rows, small_rows)]
                out[pl.ds(at, small_rows), pl.ds(i * half, half)] = part

        for i, scatter in enumerate(scatters):
            part = pl.ds(i * rows, rows)
            if scatter.by_rows:
                out[part] = ins.pop(0)[...]
                continue
            for turn, core in enumerate((spot.core, 1 - spot.core)):
                ref = ins.pop(0)
                out[part, rows_at(core * half, half)] = ref[pl.ds(0, rows)]
                if turn == 1 and scatter.small is not None:
                    small(ref, count * rows + small_rows)
        for ref in ins:
            small(ref, count * rows)

    whole = ((count * rows + 2 * small_rows, width), BF16)
    (joined,) = call(run, [(VMEM, array) for array in given], [(VMEM,) + whole], [], name)
    return joined


def collect_kernel(group, turns, n_started, *refs):
    arrays, refs = refs[: len(turns)], refs[len(turns) + n_started :]
    (*outs, held, high, copies) = refs
    spot = Spot()
    rows, width = held.shape[1:]
    parts = []
    for i, (layer, by_rows) in enumerate(group):
        part = pl.ds(i * rows, rows)
        for source, turn in zip(arrays, turns):
            quarter = spot.block(turn)
            if by_rows:
                target = outs[1].at[layer, rows_at(quarter * rows, rows), :]
            else:
                target = outs[0].at[layer, :, rows_at(quarter * width, width)]
            parts.append((copies.start(source.at[part], held.at[len(parts)]), target))
    leaving = []
    for i, (copy, target) in enumerate(parts):
        copy.wait()
        high[i] = held[i].astype(F32)
        leaving.append(copies.start(high.at[i], target))
    return leaving


def norm(values):
    center = jnp.mean(values, axis=-1, keepdims=True)
    offsets = values - center
    inverse = lax.rsqrt(jnp.mean(offsets * offsets, axis=-1, keepdims=True) + 1e-05)
    return offsets * inverse, inverse


def norm_back(upstream, unit, inverse, gain):
    scaled = upstream * gain
    center = jnp.mean(scaled, axis=-1, keepdims=True)
    along = jnp.mean(scaled * unit, axis=-1, keepdims=True)
    return inverse * (scaled - center - unit * along)


def gelu_both(v):
    scale = math.sqrt(2.0 / math.pi)
    square = v * v
    half = 0.5 + 0.5 * jnp.tanh(v * (scale + (scale * 0.044715) * square))
    spread = (2.0 * half) * (1.0 - half)
    return v * half, half + (v * spread) * (scale + (3.0 * scale * 0.044715) * square)


def mix_forward(rows, hid, seq, gain, shift, real, imag, outs):
    unit, inverse, normed_low = outs
    hid_cos, hid_sin = hid[0](), hid[1]()

    @row_steps(rows.shape[0])
    def _(at):
        real[at, :] = dot(rows[at, :], hid_cos[...]).astype(BF16)
        imag[at, :] = dot(rows[at, :], hid_sin[...]).astype(BF16)

    seq_cos, seq_sin = seq[0](), seq[1]()

    @row_steps(rows.shape[0])
    def _(at):
        mixed = dot(seq_cos[at, :], real[...]) - dot(seq_sin[at, :], imag[...])
        unit_rows, inverse_rows = norm(rows[at, :].astype(F32) + mixed)
        unit.buffer[at, :] = unit_rows
        inverse[at, :] = inverse_rows
        normed_low.buffer[at, :] = (unit_rows * gain[...] + shift[...]).astype(BF16)
        normed_low.push(at)
        unit.push(at)


def first_mix_kernel(numbers, boundary, received, hid_cos, hid_sin, cos_tiles, sin_tiles, gain, shift, *refs):
    seq_cos, seq_sin = refs[0:2]
    outs, (rows, real, imag, copies) = refs[2:5], refs[5:]
    chosen = choose(copies, boundary.at[0, pl.ds(0, rows.shape[0])], received, rows)
    cos_tiles, sin_tiles = cos_tiles(), sin_tiles()
    base = cos_tiles.shape[1]
    slots = seq_cos.buffer.shape[0] // base
    for i in range(slots):
        for j in range(slots):
            window = (pl.ds(i * base, base), pl.ds(j * base, base))
            number = numbers[i * slots + j]
            seq_cos.buffer[window] = cos_tiles[number]
            seq_sin.buffer[window] = sin_tiles[number]
    seq_cos.push()
    seq_sin.push()
    seq = (lambda: seq_cos.buffer, lambda: seq_sin.buffer)
    chosen.wait()
    mix_forward(rows, (hid_cos, hid_sin), seq, gain, shift, real, imag, outs)


def expand_kernel(layer, by_permutes, n_sources, normed, other_normed, b_in, *refs):
    sources, (hidden, slope, whole, copies) = refs[:n_sources], refs[n_sources:]
    scratch = whole.buffer
    loaded = load_in(layer, sources, scratch, copies)
    spot = Spot(by_permutes)
    width = scratch.shape[2]
    count = normed.buffer.shape[0]
    for pair in range(2):
        biases = [b_in[:, rows_at(spot.block(2 * pair + i) * (width // 2), width // 2)] for i in range(2)]
        bias = jnp.concatenate(biases, axis=1)
        for copy in loaded[pair]:
            copy.wait()
        whole.push(pair)
        for place, rows in enumerate((normed, other_normed)):
            rows = rows()

            @row_steps(count)
            def _(at):
                value, rate = gelu_both(dot(rows[at, :], scratch[pair]) + bias)
                to = pl.ds(place * count + at.start, at.size)
                hidden.buffer[pair, to, :] = value.astype(BF16)
                slope.buffer[pair, to, :] = rate.astype(BF16)

        hidden.push(pair)
        slope.push(pair)


def contract_kernel(layer, n_sources, hidden, *refs):
    sources, (own, other, whole, copies) = refs[:n_sources], refs[n_sources:]
    scratch = whole.buffer
    loaded = load_out(layer, sources, scratch, copies)
    count, width = own.buffer.shape[0], hidden.buffer.shape[2]
    for copy in loaded:
        copy.wait()
    whole.push()
    for place, out in ((1, other), (0, own)):

        @row_steps(count)
        def _(at):
            rows = pl.ds(place * count + at.start, at.size)
            hidden(1)
            held = hidden.buffer
            total = dot(held[0, rows, :], scratch[0:width, :]) + dot(held[1, rows, :], scratch[width:, :])
            out.buffer[at, :] = total.astype(out.buffer.dtype)
            out.push(at)


def second_norm(at, own, received, unit_one, gain_one, shift_one, b_out):
    normed = unit_one[at, :] * gain_one[...] + shift_one[...]
    return norm(normed + (own[at, :] + received[at, :].astype(F32) + b_out[...]))


def middle_kernel(own, received, unit_one, gain_one, shift_one, b_out, gain_two, shift_two, *refs):
    hid, seq, (next_gain, next_shift) = refs[:2], refs[2:4], refs[4:6]
    unit_two, inverse_two = refs[6:8]
    outs, (mid, real, imag, _) = refs[8:11], refs[11:]
    own, received, unit_one = own(), received(), unit_one()

    @row_steps(mid.shape[0])
    def _(at):
        unit, inverse = second_norm(at, own, received, unit_one, gain_one, shift_one, b_out)
        unit_two.buffer[at, :] = unit
        inverse_two[at, :] = inverse
        mid[at, :] = (unit * gain_two[...] + shift_two[...]).astype(BF16)

    unit_two.push()
    mix_forward(mid, hid, seq, next_gain, next_shift, real, imag, outs)


def second_back(at, upstream, unit, inverse, gain, d_second, branch_grad, small):
    grad = norm_back(upstream, unit, inverse, gain[...])
    low = grad.astype(BF16)
    branch_grad.buffer[at, :] = low
    branch_grad.push(at)
    d_second.buffer[at, :] = grad
    d_second.push(at)
    small[0:1, :] += column_sum(low.astype(F32))
    small[1:2, :] += column_sum(upstream * unit)
    small[2:3, :] += column_sum(upstream)


def turn_kernel(own, received, unit_one, gain_one, shift_one, b_out, gain_two, shift_two, *refs):
    boundary, given, out_rows, d_second, branch_grad, small, cotangent, copies = refs
    count = cotangent.shape[0]
    chosen = choose(copies, given, boundary.at[0, pl.ds(count, count)], cotangent)
    own, received, unit_one = own(), received(), unit_one()
    small[...] = jnp.zeros_like(small)
    chosen.wait()

    @row_steps(own.shape[0])
    def _(at):
        unit, inverse = second_norm(at, own, received, unit_one, gain_one, shift_one, b_out)
        out_rows.buffer[at, :] = (unit * gain_two[...] + shift_two[...]).astype(BF16)
        upstream = cotangent[at, :].astype(F32)
        second_back(at, upstream, unit, inverse, gain_two, d_second, branch_grad, small)
        out_rows.push(at)


def grad_out_kernel(by_permutes, hidden, branch_grad, other_grad, *refs):
    outs, (tiles, copies) = refs[:-2], refs[-2:]
    spot = Spot(by_permutes)
    count = branch_grad.shape[0]
    shard = tiles.shape[1]
    for turn in range(BLOCKS):
        columns = pl.ds((turn % 2) * shard, shard)
        grad = 0.0
        for i, ref in enumerate((branch_grad, other_grad)):
            rows = hidden[turn // 2, pl.ds(i * count, count), columns]
            grad = grad + dot(rows, ref[...], ((0,), (0,)))
        if not by_permutes:
            outs[0][pl.ds(turn * shard, shard), :] = grad.astype(BF16)
            continue
        tiles[turn] = grad.astype(BF16)
        rows = outs[0].shape[2]
        apart = spot.block(turn) ^ spot.chip
        for slot in range(BLOCKS):
            part = tiles[turn, rows_at(spot.block(slot) * rows, rows), :]
            outs[slot // 2][slot % 2, apart] = part


def shrink_kernel(by_permutes, n_outs, branch_grad, other_grad, slope, normed, other_normed, whole_out, whole_in, *refs):
    outs, (b_grad, own, other, tiles, act_grad, copies) = refs[:n_outs], refs[n_outs:]
    spot = Spot(by_permutes)
    count = branch_grad.shape[0]
    width = tiles.shape[2]
    half = width // 2
    b_grad[...] = jnp.zeros_like(b_grad)
    for pair in range(2):
        sums = []
        for place, ref in enumerate((branch_grad, other_grad)):

            @row_steps(count)
            def _(at):
                rows = pl.ds(place * count + at.start, at.size)
                grad = dot(ref[at, :], whole_out[pl.ds(pair * width, width), :], ((1,), (1,)))
                low = (grad * slope[pair, rows, :].astype(F32)).astype(BF16)
                act_grad[pair, rows, :] = low
                sums.append(column_sum(low.astype(F32)))

        total = sum(sums[1:], sums[0])
        for side in range(2):
            block = spot.block(2 * pair + side)
            b_grad[:, rows_at((2 * block + spot.core) * half, half)] = total[:, side * half : (side + 1) * half]

        @row_steps(tiles.shape[1])
        def _(at):
            grad = 0.0
            for place, ref in enumerate((normed, other_normed)):
                grads = act_grad[pair, pl.ds(place * count, count), :]
                grad = grad + dot(ref[:, at], grads, ((0,), (0,)))
            if by_permutes:
                tiles[pair, at, :] = grad.astype(BF16)
            else:
                outs[0][at, pl.ds(pair * width, width)] = grad.astype(BF16)

        if by_permutes:
            rows = outs[0].shape[2]
            for side in range(2):
                for chip in range(spot.chips):
                    part = tiles[pair, pl.ds(chip * rows, rows), pl.ds(side * half, half)]
                    outs[pair][side, chip ^ spot.chip] = part
    for place, out in ((1, other), (0, own)):

        @row_steps(count)
        def _(at):
            rows = pl.ds(place * count + at.start, at.size)
            total = dot(act_grad[0, rows, :], whole_in[0], ((1,), (1,)))
            total = total + dot(act_grad[1, rows, :], whole_in[1], ((1,), (1,)))
            out[at, :] = total.astype(out.dtype)


def unmix(refs, total, mix_grad, real, imag, small, input_grad):
    own, received, d_second, unit_one, inverse_one, gain_one, hid_cos, hid_sin, seq_cos, seq_sin = refs
    own, received, d_second, unit_one = own(), received(), d_second(), unit_one()
    small[...] = jnp.zeros_like(small)

    @row_steps(total.shape[0])
    def _(at):
        upstream = d_second[at, :] + own[at, :] + received[at, :].astype(F32)
        unit = unit_one[at, :]
        grad = norm_back(upstream, unit, inverse_one[at, :], gain_one[...])
        total[at, :] = grad
        mix_grad[at, :] = grad.astype(BF16)
        small[0:1, :] += column_sum(upstream * unit)
        small[1:2, :] += column_sum(upstream)

    seq_cos, seq_sin = seq_cos(), seq_sin()

    @row_steps(total.shape[0])
    def _(at):
        real[at, :] = dot(seq_cos[at, :], mix_grad[...]).astype(BF16)
        imag[at, :] = (-dot(seq_sin[at, :], mix_grad[...])).astype(BF16)

    hid_cos, hid_sin = hid_cos(), hid_sin()

    @row_steps(total.shape[0])
    def _(at):
        grad = dot(real[at, :], hid_cos[...]) + dot(imag[at, :], hid_sin[...])
        input_grad(at, total[at, :] + grad)


def last_kernel(*refs):
    ins, (out_rows, *smalls) = refs[:10], refs[10:17]
    sent, kept, packed, total, mix_grad, real, imag, small, _ = refs[17:]
    is_first = lax.axis_index("section") % 2 == 0
    rows = out_rows()

    def input_grad(at, values):
        low = values.astype(BF16)
        sent.buffer[at, :] = jnp.where(is_first, rows[at, :], low)
        kept.buffer[at, :] = jnp.where(is_first, low, rows[at, :])
        sent.push(at)
        kept.push(at)

    unmix(ins, total, mix_grad, real, imag, small, input_grad)
    width = packed.shape[1]
    packed[...] = jnp.zeros_like(packed)
    for layer in range(2):
        b_grad, sums_two = smalls[3 * layer : 3 * layer + 2]
        sums_one = smalls[3 * layer + 2] if layer else small
        at = layer * (packed.shape[0] // 2)
        sums = (sums_two[0:1], sums_one[0:1], sums_one[1:2], sums_two[1:2], sums_two[2:3])
        for vector in (b_grad[...],) + sums:
            for i in range(vector.shape[1] // width):
                packed[at : at + 1, :] = vector[:, i * width : (i + 1) * width].astype(packed.dtype)
                at += 1


def finish_kernel(kept, back, result, held, high, copies):
    layer = lax.axis_index("section") % 2
    count = held.shape[1]
    arriving = [copies.start(ref, held.at[i]) for i, ref in enumerate((kept, back))]
    leaving = []
    for i, block in enumerate((layer, 1 - layer)):
        arriving[i].wait()
        high[i] = held[i].astype(F32)
        leaving.append(copies.start(high.at[i], result.at[0, rows_at(block * count, count)]))
    return leaving


def relay_kernel(*refs):
    ins, (unit_two, inverse_two, gain_two) = refs[:10], refs[10:13]
    small, d_second, branch_grad, small_two, total, mix_grad, real, imag, _ = refs[13:]
    small_two[...] = jnp.zeros_like(small_two)

    def input_grad(at, values):
        upstream = values.astype(BF16).astype(F32)
        unit = unit_two()[at, :]
        second_back(at, upstream, unit, inverse_two[at, :], gain_two, d_second, branch_grad, small_two)

    unmix(ins, total, mix_grad, real, imag, small, input_grad)


def body(boundary, bucket_ids, w_in, b_in, w_out, b_out, gain_one, shift_one, gain_two, shift_two):
    place = Place()
    Order.begin()
    layers = w_in.shape[0]
    micro_count = bucket_ids.shape[1]
    feat_width = boundary.shape[2]
    ff_width = w_in.shape[2]
    slab_len = boundary.shape[1] // micro_count
    slots = bucket_ids.shape[2]
    base_len = slab_len // slots
    half_block = ff_width // (2 * BLOCKS)
    by_permutes = place.n_section == 4 and place.chips == 4
    last = layers - 1

    bucket_row = bucket_ids[place.section // 2, place.section % 2]
    half_bias = lax.dynamic_index_in_dim(
        b_in.reshape(layers, BLOCKS, 2, half_block), place.core, 2, keepdims=False
    ).reshape(layers, -1)

    block = (slab_len, feat_width)
    both = (2 * slab_len, feat_width)
    wide_block = (2, 2 * slab_len, ff_width // 4)
    whole_in_shape = (2, feat_width, ff_width // 4)
    whole_out_shape = (ff_width // 2, feat_width)
    column = (VMEM, (slab_len, 1), F32)
    sums_shape = (VMEM, (8, feat_width), F32)
    mix_outs = [(EARLY, block, F32), column, (EARLY, block, BF16)]
    hid = [(LATE, jnp.asarray(table.astype(BF16))) for table in dft_tables(feat_width)]

    def late(*arrays):
        return [(LATE, array) for array in arrays]

    def plain(*arrays):
        return [(HBM, array) for array in arrays]

    def param(array, layer):
        return (VMEM, array[layer][None])

    shard_rows, piece_rows = w_in.shape[1], w_out.shape[1] // BLOCKS
    prepared = [(HBM, block, BF16)]
    if by_permutes:
        prepared += [(HBM, (layers, shard_rows, ff_width // 2), BF16)]
        prepared += [(HBM, (piece_rows, feat_width), BF16)] * layers
    given, *prepared = call(
        partial(prepare_kernel, layers, by_permutes),
        plain(boundary, w_in, w_out),
        prepared,
        [
            (block, BF16),
            ((layers, shard_rows, ff_width // 2), BF16),
            ((layers, piece_rows, feat_width), BF16),
        ],
        "prepare",
        spare=54 * 2**20,
    )
    sources_in, sources_out = [None] * layers, [None] * layers
    if by_permutes:
        for_other, out_zero_piece, out_one_piece = prepared
        in_zero, out_zero, in_one, out_one = (
            Gather(place, name + str(layer), w, None, layer, by_rows)
            for layer in range(layers)
            for name, w, by_rows in (("in", w_in, False), ("out", w_out, True))
        )
        other_rows = place.swap_core(for_other)
        received = place.swap_layer(given)
        in_zero.other_rows = in_one.other_rows = other_rows
        out_zero_moved = place.along_z(out_zero_piece, 1)
        in_zero.shift(in_zero.join(other_rows))
        pieces_one = in_one.join(other_rows, out_one_piece)
        out_zero_pair = pack("pair_out0", [out_zero_piece, out_zero_moved])
        out_zero.moved = [out_zero_moved, place.along_z(out_zero_pair, 2)]
        Order.wait(received)
        in_zero.one()
        moved_one = place.along_z(tie(pieces_one, Order.token), 1)
    else:
        received = place.swap_layer(given)
        for layer in range(layers):
            whole_in, whole_out = (
                lax.all_gather(w[layer], "dp", axis=0, tiled=True) for w in (w_in, w_out)
            )
            whole_in = whole_in.reshape(feat_width, BLOCKS, 2, half_block)
            whole_out = whole_out.reshape(BLOCKS, 2, half_block, feat_width)
            whole_in = lax.dynamic_index_in_dim(whole_in, place.core, 2, keepdims=False)
            whole_out = lax.dynamic_index_in_dim(whole_out, place.core, 1, keepdims=False)
            sources_in[layer] = [whole_in.reshape(feat_width, -1)]
            sources_out[layer] = [whole_out.reshape(-1, feat_width)]

    numbers = tile_numbers(bucket_row, slots).reshape(-1)
    tiles = [(LATE, jnp.asarray(table)) for table in sequence_tiles(base_len)]
    seq_cos, seq_sin, *mixed = call(
        first_mix_kernel,
        [(SMEM, numbers)]
        + plain(boundary, received)
        + hid
        + tiles
        + [param(gain_one, 0), param(shift_one, 0)],
        [(EARLY, (slab_len, slab_len), BF16)] * 2 + mix_outs,
        [(block, BF16)] * 3,
        "first_mix",
    )
    tables = hid + late(seq_cos, seq_sin)

    both_pairs, all_rows = pl.ds(0, 2), pl.ds(0, 2 * slab_len)
    steps = slab_len // ROW_STEP
    row_parts = [
        (both_pairs, pl.ds(slab_len * place_ + i * ROW_STEP, ROW_STEP))
        for place_ in (1, 0)
        for i in range(steps)
    ]
    block_parts = [
        (pair, all_rows, pl.ds(side * half_block, half_block)) for pair in range(2) for side in range(2)
    ]
    pair_parts = [(pl.ds(pair, 1),) for pair in range(2)]
    half_parts = [(pl.ds(pair * 2 * half_block, 2 * half_block),) for pair in range(2)]

    saved, wholes_in, wholes_out = [], [], []
    for layer in range(layers):
        unit_one, inverse_one, normed = mixed
        if by_permutes and layer == 0:
            mark = Order.mark(in_zero.from_one, in_zero.from_two)
            in_zero.two(mark)
            other_normed = place.swap_core(tie(normed, mark))
            pair_in, pair_out = pairs(pieces_one, moved_one)
            out_zero.one()
            in_one.moved = [(pair_in, 1, 1), place.along_z(pair_in, 2)]
            sources_in[0] = in_zero.sources()
        else:
            other_normed = place.swap_core(normed)
        if by_permutes and layer == 1:
            Order.mark(in_one.far)
            mark = Order.mark(out_one.from_one, out_one.from_two)
            out_one.two(mark)
            sources_in[1] = in_one.sources()
        hidden, slope, whole_in = call(
            partial(expand_kernel, layer, by_permutes, len(sources_in[layer])),
            late(normed, other_normed)
            + [(VMEM, half_bias[layer][None])]
            + plain(*sources_in[layer]),
            [(EARLY, wide_block, BF16), (EARLY, wide_block, BF16), (EARLY, whole_in_shape, BF16)],
            [],
            "expand",
        )
        if by_permutes and layer == 0:
            mark = Order.mark(out_zero.from_one, out_zero.from_two)
            out_zero.two(mark)
            in_one.one()
            out_one.moved = [(pair_out, 1, 1), place.along_z(tie(pair_out, in_one.along), 2)]
            sources_out[0] = out_zero.sources()
        if by_permutes and layer == 1:
            sources_out[1] = out_one.sources()
        own_part, other_part, whole_out = call(
            partial(contract_kernel, layer, len(sources_out[layer])),
            [(LATE, hidden, row_parts)] + plain(*sources_out[layer]),
            [(EARLY, block, F32), (EARLY, block, BF16), (EARLY, whole_out_shape, BF16)],
            [],
            "contract",
        )
        from_other = place.swap_core(other_part)
        if by_permutes and layer == 0:
            mark = Order.mark(in_one.from_one, in_one.from_two)
            in_one.two(mark)
            out_one.one()
        wholes_in.append(whole_in)
        wholes_out.append(whole_out)
        common = late(own_part, from_other, unit_one) + [
            param(p, layer) for p in (gain_one, shift_one, b_out, gain_two, shift_two)
        ]
        kept = [unit_one, inverse_one, normed, other_normed, hidden, slope]
        if layer < last:
            unit_two, inverse_two, *mixed = call(
                middle_kernel,
                common + tables + [param(gain_one, layer + 1), param(shift_one, layer + 1)],
                [(EARLY, block, F32), column] + mix_outs,
                [(block, BF16), (block, BF16), (block, BF16)],
                "middle",
            )
            kept += [unit_two, inverse_two]
        saved.append(kept)

    Order.cost = BACKWARD_COST
    out_rows, d_second, branch_grad, sums_two = call(
        turn_kernel,
        common + plain(boundary, received),
        [(EARLY, block, BF16), (EARLY, block, F32), (EARLY, block, BF16), sums_shape],
        [(block, BF16)],
        "turn",
    )

    if by_permutes:
        piece_out = (2, place.chips, w_out.shape[1] // BLOCKS, feat_width)
        piece_in = (2, place.chips, 2 * w_in.shape[1], half_block)
        grad_outs = {True: [(VMEM, piece_out, BF16)] * 2, False: [(VMEM, piece_in, BF16)] * 2}
    else:
        grad_outs = {
            True: [(VMEM, (ff_width // 2, feat_width), BF16)],
            False: [(VMEM, (feat_width, ff_width // 2), BF16)],
        }
    n_outs = len(grad_outs[True])
    grads, smalls, running = {}, {}, []

    def reduce_grad(pieces, layer, by_rows):
        name = ("out" if by_rows else "in") + str(layer)
        if by_permutes:
            grads[layer, by_rows] = Scatter(place, name, *pieces, by_rows)
            running.append(grads[layer, by_rows])
            return
        (half,) = pieces
        if by_rows:
            whole = jnp.zeros((BLOCKS, 2, half_block, feat_width), BF16)
            half = half.reshape(BLOCKS, 1, half_block, feat_width)
            whole = lax.dynamic_update_slice_in_dim(whole, half, place.core, 1)
            whole = whole.reshape(ff_width, feat_width)
        else:
            whole = jnp.zeros((feat_width, BLOCKS, 2, half_block), BF16)
            half = half.reshape(feat_width, BLOCKS, 1, half_block)
            whole = lax.dynamic_update_slice_in_dim(whole, half, place.core, 2)
            whole = whole.reshape(feat_width, ff_width)
        part = lax.psum_scatter(whole, "dp", scatter_dimension=0, tiled=True)
        grads[layer, by_rows] = lax.psum(part, "section").astype(F32)

    for layer in reversed(range(layers)):
        unit_one, inverse_one, normed, other_normed, hidden, slope = saved[layer][:6]
        other_grad = place.swap_core(branch_grad)
        if by_permutes and layer == 0:
            running[0].two()
            running[1].two()
        pieces = call(
            partial(grad_out_kernel, by_permutes),
            [(VMEM, hidden), (VMEM, branch_grad), (VMEM, other_grad)],
            grad_outs[True],
            [((BLOCKS, half_block, feat_width), BF16)],
            "grad_out",
        )
        reduce_grad(pieces, layer, True)
        if by_permutes and layer == 0:
            running[0].three()
            Order.mark(running[1].from_two)
        *pieces, b_grad, own_part, other_part = call(
            partial(shrink_kernel, by_permutes, n_outs),
            [
                (VMEM, array)
                for array in (branch_grad, other_grad, slope, normed, other_normed)
                + (wholes_out[layer], wholes_in[layer])
            ],
            grad_outs[False]
            + [(VMEM, (1, ff_width), F32), (VMEM, block, F32), (VMEM, block, BF16)],
            [((2, feat_width, ff_width // 4), BF16), (wide_block, BF16)],
            "shrink",
        )
        from_other = place.swap_core(other_part)
        reduce_grad(pieces, layer, False)
        if by_permutes and layer == last:
            Order.mark(running[0].from_one)
        if by_permutes and layer == 0:
            running[0].neighbour()
            running[2].two()
            running[1].three()
        ins = (
            late(own_part, from_other, d_second, unit_one)
            + [(VMEM, inverse_one), param(gain_one, layer)]
            + tables
        )
        work = [(block, F32), (block, BF16), (block, BF16), (block, BF16)]
        smalls[layer] = [b_grad, sums_two]
        if layer > 0:
            below_unit, below_inverse = saved[layer - 1][6:8]
            sums_one, d_second, branch_grad, sums_two = call(
                relay_kernel,
                ins + late(below_unit) + [(VMEM, below_inverse), param(gain_two, layer - 1)],
                [sums_shape, (EARLY, block, F32), (EARLY, block, BF16), sums_shape],
                work,
                "relay",
            )
            smalls[layer].append(sums_one)
    vectors = smalls[0] + [smalls[1][2]] + smalls[1]
    small_type = BF16 if by_permutes else F32
    sent, kept_rows, packed = call(
        last_kernel,
        ins + late(out_rows) + [(VMEM, vector) for vector in vectors],
        [(EARLY, block, BF16), (EARLY, block, BF16), (VMEM, (64, half_block), small_type)],
        work + [((8, feat_width), F32)],
        "last",
    )

    def finish():
        return call(
            finish_kernel,
            plain(kept_rows, back),
            [(HBM, (1, 2 * slab_len, feat_width), F32)],
            [((2,) + block, BF16), ((2,) + block, F32)],
            "finish",
        )

    if by_permutes:

        def share(mine):
            return [place.plane_one(mine), place.plane_two(mine)]

        out_last, in_last, out_first, in_first = running
        in_first.small = [(packed, pl.ds(0, packed.shape[0]))]
        out_first.three()
        in_first.two()
        out_last.four()
        in_last.neighbour()
        in_first.three()
        back = place.swap_layer(tie(sent, Order.token))
        in_last.four()
        out_first.neighbour()
        in_first.neighbour()
        (result,) = finish()
        mine = join("join_rest", [in_last, out_last])
        rest = share(mine)
        out_first.four()
        in_first.four()
        rest.append(place.plane_two(tie(rest[0], Order.token)))
        Order.wait(rest[1])
        last_mine = join("join_last", [in_first, out_first])
        last_rest = share(last_mine)
        groups = [[(last, False), (last, True)], [(0, False), (0, True)]]
        unit = (shard_rows, ff_width // BLOCKS)

        def collect(group, quarters, started):
            turns, arrays = zip(*quarters)
            held = ((len(turns) * len(group),) + unit,)
            n = len(turns)
            return call(
                partial(collect_kernel, group, turns, len(started)),
                plain(*arrays, *started),
                [(HBM, w_in.shape, F32), (HBM, w_out.shape, F32)],
                [held + (BF16,), held + (F32,)],
                "collect",
                aliases={n: 0, n + 1: 1} if started else None,
            )

        Order.wait(rest[2])
        started = collect(groups[0], zip((3, 0, 2, 1), [mine] + rest), ())
        mark = Order.mark(*last_rest)
        far = place.plane_two(tie(last_rest[0], mark))
        started = collect(groups[1], zip((3, 0, 2), [last_mine] + last_rest), tuple(started))
        at, size = 2 * shard_rows, (last_mine.shape[0] - 2 * shard_rows) // 2
        packed = sum(
            array[at + i * size : at + (i + 1) * size].astype(F32)
            for i, arrays in enumerate(((last_mine, last_rest[0]), (last_mine, last_rest[1])))
            for array in arrays
        )
        packed = packed.reshape(-1, 2, half_block).transpose(1, 0, 2).reshape(-1, half_block)
        packed = tie(packed, Order.token)
        Order.wait(packed)
        grad_in, grad_out = collect(groups[1], [(1, far)], tuple(started))
    else:
        back = place.swap_layer(sent)
        grad_in, grad_out = (
            jnp.stack([grads[layer, by_rows] for layer in range(layers)])
            for by_rows in (False, True)
        )
        packed = lax.psum(packed, AXES)
        (result,) = finish()
    b_part, part = ff_width // place.n_dp, feat_width // place.n_dp
    flat = packed.reshape(layers, -1)
    small_out = [lax.dynamic_slice_in_dim(flat, place.dp * b_part, b_part, 1)]
    sums = flat[:, ff_width : ff_width + 5 * feat_width].reshape(layers, 5, feat_width)
    sums = lax.dynamic_slice_in_dim(sums, place.dp * part, part, 2)
    small_out += [sums[:, i] for i in range(5)]
    return (result, grad_in, small_out[0], grad_out, *small_out[1:])


def solution(mesh):
    return jax.shard_map(
        body,
        mesh=mesh,
        in_specs=(
            P("section", "dp", None),
            P(None, "dp", None),
            P(None, "dp", None),
            P(),
            P(None, "dp", None),
            P(),
            P(),
            P(),
            P(),
            P(),
        ),
        out_specs=(
            P("section", "dp", None),
            P(None, "dp", None),
            P(None, "dp"),
            P(None, "dp", None),
            P(None, "dp"),
            P(None, "dp"),
            P(None, "dp"),
            P(None, "dp"),
            P(None, "dp"),
        ),
        check_vma=False,
    )
```

profile of v0, /device:TPU:0, one launch (start us, length us, event | category | flops | bytes accessed | tf_op | source)
XLA Modules:
  0.0 268.8 jit_solution(4016580406233988507)
XLA Ops:
  1.3 3.3 %prepare.1 = (bf16[512,768]{1,0:T(8,128)(2,1)}, bf16[2,96,1536]{2,1,0:T(8,128)(2,1)}, bf16[96,768]{1,0:T(8,128)(2,1)}, bf16[96,768]{1,0:T(8,128)(2,1)}, f32[8,128]{1,0:T(8,128)}) custom-call(bf16[1,1024,768]{2,1,0:T(8,128)(2,1)} %refs_8_.2, bf16[2,96,3072]{2,1,0:T(8,128)(2,1)} %refs_3_.4, bf16[2,384,768]{2,1,0:T(8,128)(2,1)} %refs_1_.7, ...), custom_call_target="tpu_custom_call" | custom-call | flops 10000000000 | bytes 1000 | tf_op jit(solution)/shard_map/prepare/pallas_call | solution.py:243
  18.2 9.3 %collective-permute-done.refs_2_.refs_9_ = bf16[512,768]{1,0:T(8,128)(2,1)S(1)} collective-permute-done((bf16[512,768]{1,0:T(8,128)(2,1)}, bf16[512,768]{1,0:T(8,128)(2,1)S(1)}, u32[]{:S(2)}, u32[]{:S(2)}) %collective-permute-start) | collective-permute-done | bytes 786464 | tf_op jit(solution)/shard_map/ppermute | solution.py:42
  27.7 5.1 %collective-permute-start.6 = (bf16[3,192,384]{2,1,0:T(8,128)(2,1)S(1)}, bf16[3,192,384]{2,1,0:T(8,128)(2,1)S(1)}, u32[]{:S(2)}, u32[]{:S(2)}) collective-permute-start(bf16[3,192,384]{2,1,0:T(8,128)(2,1)S(1)} %get-tuple-element.175.refs_5_), channel_id=1, source_target_pairs={{0,8},{1,17},{2,10},{3,19},{4,12},{5,21},{6,14},{7,23},{8,0},{9,25... | collective-permute-start | bytes 1327112 | tf_op jit(solution)/shard_map/ppermute | solution.py:42
  34.3 3.7 %collective-permute-start.11 = (bf16[2,96,768]{2,1,0:T(8,128)(2,1)S(1)}, bf16[2,96,768]{2,1,0:T(8,128)(2,1)S(1)}, u32[]{:S(2)}, u32[]{:S(2)}) collective-permute-start(bf16[2,96,768]{2,1,0:T(8,128)(2,1)S(1)} %get-tuple-element.181.refs_0_), channel_id=1, source_target_pairs={{0,2},{1,3},{2,0},{3,1},{4,6},{5,7},{6,4},{7,5},{8,10},{9,11},{10,... | collective-permute-start | bytes 884744 | tf_op jit(solution)/shard_map/ppermute | solution.py:42
  38.0 3.4 %first_mix.1 = (bf16[512,512]{1,0:T(8,128)(2,1)S(1)}, bf16[512,512]{1,0:T(8,128)(2,1)S(1)}, f32[512,768]{1,0:T(8,128)S(1)}, f32[512,1]{1,0:T(8,128)S(1)}, bf16[5...) custom-call(s32[16]{0:T(128)S(1)} %select_n.89.refs_0_, bf16[1,1024,768]{2,1,0:T(8,128)(2,1)S(1)} %copy-done.2, ...), custom_call_target="tpu_custom_call" | custom-call | flops 10000000000 | bytes 1000 | tf_op jit(solution)/shard_map/first_mix/pallas_call | solution.py:243
  42.7 3.6 %collective-permute-done.11.refs_1_ = bf16[2,96,768]{2,1,0:T(8,128)(2,1)S(1)} collective-permute-done((bf16[2,96,768]{2,1,0:T(8,128)(2,1)S(1)}, bf16[2,96,768]{2,1,0:T(8,128)(2,1)S(1)}, u32[]{:S(2)}, u32[]{:S(2)}) %collective-permute-start.11) | collective-permute-done | bytes 294944 | tf_op jit(solution)/shard_map/ppermute | solution.py:42
  51.7 5.8 %expand.2 = (bf16[2,1024,768]{2,1,0:T(8,128)(2,1)S(1)}, bf16[2,1024,768]{2,1,0:T(8,128)(2,1)S(1)}, bf16[2,768,768]{2,1,0:T(8,128)(2,1)S(1)}, f32[8,128]{1,0:T(8,128)S(1)}) custom-call(bf16[512,768]{1,0:T(8,128)(2,1)S(1)} %get-tuple-element.177.refs_0_.refs_3_, bf16[512,768]{1,0:T(8,128)(2,1)S(1)} %collective-permute-done.8.refs_1_.refs_4_, ...), custom_call_target="tpu_custom_call" | custom-call | flops 10000000000 | bytes 1000 | tf_op jit(solution)/shard_map/expand/pallas_call | solution.py:243
  60.5 4.6 %collective-permute-done.15.refs_1_ = bf16[2,192,384]{2,1,0:T(8,128)(2,1)S(1)} collective-permute-done((bf16[2,192,384]{2,1,0:T(8,128)(2,1)S(1)}, bf16[2,192,384]{2,1,0:T(8,128)(2,1)S(1)}, u32[]{:S(2)}, u32[]{:S(2)}) %collective-permute-start.15) | collective-permute-done | bytes 294944 | tf_op jit(solution)/shard_map/ppermute | solution.py:42
  70.4 5.2 %contract.2 = (f32[512,768]{1,0:T(8,128)S(1)}, bf16[512,768]{1,0:T(8,128)(2,1)S(1)}, bf16[1536,768]{1,0:T(8,128)(2,1)S(1)}, f32[8,128]{1,0:T(8,128)S(1)}) custom-call(bf16[2,1024,768]{2,1,0:T(8,128)(2,1)S(1)} %get-tuple-element.184.refs_0_, bf16[2,384,768]{2,1,0:T(8,128)(2,1)S(1)} %copy-done.4, bf16[3,96,768]{2,1,0:T(8,128)(2,1)S(1)} %get-tuple-element.185.refs_2_, ...), custom_call_target="tpu_custom_call" | custom-call | flops 10000000000 | bytes 1000 | tf_op jit(solution)/shard_map/contract/pallas_call | solution.py:243
  77.5 3.9 %collective-permute-done.17.refs_1_ = bf16[2,96,768]{2,1,0:T(8,128)(2,1)S(1)} collective-permute-done((bf16[2,96,768]{2,1,0:T(8,128)(2,1)S(1)}, bf16[2,96,768]{2,1,0:T(8,128)(2,1)S(1)}, u32[]{:S(2)}, u32[]{:S(2)}) %collective-permute-start.17) | collective-permute-done | bytes 294944 | tf_op jit(solution)/shard_map/ppermute | solution.py:42
  84.5 3.2 %middle.1 = (f32[512,768]{1,0:T(8,128)S(1)}, f32[512,1]{1,0:T(8,128)S(1)}, f32[512,768]{1,0:T(8,128)S(1)}, f32[512,1]{1,0:T(8,128)S(1)}, bf16[512,768]{1,0:T(8,128)(2,1)S(1)}, /*index=5*/f32[8,128]{1,0:T(8,128)S(1)}) custom-call(f32[512,768]{1,0:T(8,128)S(1)} %get-tuple-element.191.refs_0_, bf16[512,768]{1,0:T(8,128)(2,1)S(1)} %collective-permute-done.16.refs_1_, ...), custom_call_target="tpu_custom_call" | custom-call | flops 10000000000 | bytes 1000 | tf_op jit(solution)/shard_map/middle/pallas_call | solution.py:243
  87.7 10.6 %collective-permute-done.21.refs_8_ = bf16[3,192,384]{2,1,0:T(8,128)(2,1)S(1)} collective-permute-done((bf16[3,192,384]{2,1,0:T(8,128)(2,1)S(1)}, bf16[3,192,384]{2,1,0:T(8,128)(2,1)S(1)}, u32[]{:S(2)}, u32[]{:S(2)}) %collective-permute-start.21) | collective-permute-done | bytes 442400 | tf_op jit(solution)/shard_map/ppermute | solution.py:42
  101.1 5.8 %expand.3 = (bf16[2,1024,768]{2,1,0:T(8,128)(2,1)S(1)}, bf16[2,1024,768]{2,1,0:T(8,128)(2,1)S(1)}, bf16[2,768,768]{2,1,0:T(8,128)(2,1)S(1)}, f32[8,128]{1,0:T(8,128)S(1)}) custom-call(bf16[512,768]{1,0:T(8,128)(2,1)S(1)} %get-tuple-element.202.refs_0_.refs_3_, bf16[512,768]{1,0:T(8,128)(2,1)S(1)} %collective-permute-done.20.refs_1_.refs_4_, ...), custom_call_target="tpu_custom_call" | custom-call | flops 10000000000 | bytes 1000 | tf_op jit(solution)/shard_map/expand/pallas_call | solution.py:243
  107.6 5.2 %contract.3 = (f32[512,768]{1,0:T(8,128)S(1)}, bf16[512,768]{1,0:T(8,128)(2,1)S(1)}, bf16[1536,768]{1,0:T(8,128)(2,1)S(1)}, f32[8,128]{1,0:T(8,128)S(1)}) custom-call(bf16[2,1024,768]{2,1,0:T(8,128)(2,1)S(1)} %get-tuple-element.208.refs_0_, bf16[2,384,768]{2,1,0:T(8,128)(2,1)S(1)} %copy-done.4, bf16[3,96,768]{2,1,0:T(8,128)(2,1)S(1)} %get-tuple-element.206.refs_2_, ...), custom_call_target="tpu_custom_call" | custom-call | flops 10000000000 | bytes 1000 | tf_op jit(solution)/shard_map/contract/pallas_call | solution.py:243
  119.7 2.9 %grad_out.2 = (bf16[2,4,96,768]{3,2,1,0:T(8,128)(2,1)S(1)}, bf16[2,4,96,768]{3,2,1,0:T(8,128)(2,1)S(1)}, f32[8,128]{1,0:T(8,128)S(1)}) custom-call(bf16[2,1024,768]{2,1,0:T(8,128)(2,1)S(1)} %get-tuple-element.208.refs_0_, bf16[512,768]{1,0:T(8,128)(2,1)S(1)} %get-tuple-element.215.refs_1_.refs_0_, ...), custom_call_target="tpu_custom_call" | custom-call | flops 10000000000 | bytes 1000 | tf_op jit(solution)/shard_map/grad_out/pallas_call | solution.py:243
  123.7 8.2 %shrink.2 = (bf16[2,4,192,384]{3,2,1,0:T(8,128)(2,1)S(1)}, bf16[2,4,192,384]{3,2,1,0:T(8,128)(2,1)S(1)}, f32[1,3072]{1,0:T(1,128)S(1)}, f32[512,768]{1,0:T(8,128...) custom-call(bf16[512,768]{1,0:T(8,128)(2,1)S(1)} %get-tuple-element.215.refs_1_.refs_0_, ...), custom_call_target="tpu_custom_call" | custom-call | flops 10000000000 | bytes 1000 | tf_op jit(solution)/shard_map/shrink/pallas_call | solution.py:243
  133.1 5.8 %collective-permute-done.28.refs_1_ = bf16[2,4,96,768]{3,2,1,0:T(8,128)(2,1)S(1)} collective-permute-done((bf16[2,4,96,768]{3,2,1,0:T(8,128)(2,1)S(1)}, bf16[2,4,96,768]{3,2,1,0:T(8,128)(2,1)S(1)}, u32[]{:S(2)}, u32[]{:S(2)}) %collective-permute-start.28) | collective-permute-done | bytes 1179680 | tf_op jit(solution)/shard_map/ppermute | solution.py:42
  140.3 4.1 %relay.1 = (f32[8,768]{1,0:T(8,128)S(1)}, f32[512,768]{1,0:T(8,128)S(1)}, bf16[512,768]{1,0:T(8,128)(2,1)S(1)}, f32[8,768]{1,0:T(8,128)S(1)}, f32[8,128]{1,0:T(8,128)S(1)}) custom-call(f32[512,768]{1,0:T(8,128)S(1)} %get-tuple-element.221.refs_0_, bf16[512,768]{1,0:T(8,128)(2,1)S(1)} %collective-permute-done.27.refs_1_, ...), custom_call_target="tpu_custom_call" | custom-call | flops 10000000000 | bytes 1000 | tf_op jit(solution)/shard_map/relay/pallas_call | solution.py:243
  145.6 9.6 %collective-permute-done.31.refs_1_ = bf16[2,4,192,384]{3,2,1,0:T(8,128)(2,1)S(1)} collective-permute-done((bf16[2,4,192,384]{3,2,1,0:T(8,128)(2,1)S(1)}, bf16[2,4,192,384]{3,2,1,0:T(8,128)(2,1)S(1)}, u32[]{:S(2)}, u32[]{:S(2)}) %collective-permute-start.31) | collective-permute-done | bytes 1179680 | tf_op jit(solution)/shard_map/ppermute | solution.py:42
  157.1 2.9 %grad_out.3 = (bf16[2,4,96,768]{3,2,1,0:T(8,128)(2,1)S(1)}, bf16[2,4,96,768]{3,2,1,0:T(8,128)(2,1)S(1)}, f32[8,128]{1,0:T(8,128)S(1)}) custom-call(bf16[2,1024,768]{2,1,0:T(8,128)(2,1)S(1)} %copy-done.15, bf16[512,768]{1,0:T(8,128)(2,1)S(1)} %get-tuple-element.230.refs_1_.refs_0_, bf16[512,768]{1,0:T(8,128)(2,1)S(1)} %collective-permute-done.29.refs_2_.refs_1_, ...), custom_call_target="tpu_custom_call" | custom-call | flops 10000000000 | bytes 1000 | tf_op jit(solution)/shard_map/grad_out/pallas_call | solution.py:243
  160.2 5.1 %collective-permute-done.32.refs_2_ = bf16[768,384]{1,0:T(8,128)(2,1)S(1)} collective-permute-done((bf16[768,384]{1,0:T(8,128)(2,1)S(1)}, bf16[768,384]{1,0:T(8,128)(2,1)S(1)}, u32[]{:S(2)}, u32[]{:S(2)}) %collective-permute-start.32) | collective-permute-done | bytes 589856 | tf_op jit(solution)/shard_map/ppermute | solution.py:42
  168.3 8.4 %shrink.3 = (bf16[2,4,192,384]{3,2,1,0:T(8,128)(2,1)S(1)}, bf16[2,4,192,384]{3,2,1,0:T(8,128)(2,1)S(1)}, f32[1,3072]{1,0:T(1,128)S(1)}, f32[512,768]{1,0:T(8,128...) custom-call(bf16[512,768]{1,0:T(8,128)(2,1)S(1)} %get-tuple-element.230.refs_1_.refs_0_, ...), custom_call_target="tpu_custom_call" | custom-call | flops 10000000000 | bytes 1000 | tf_op jit(solution)/shard_map/shrink/pallas_call | solution.py:243
  177.2 3.3 %collective-permute-done.35.refs_3_ = bf16[192,768]{1,0:T(8,128)(2,1)S(1)} collective-permute-done((bf16[192,768]{1,0:T(8,128)(2,1)S(1)}, bf16[192,768]{1,0:T(8,128)(2,1)S(1)}, u32[]{:S(2)}, u32[]{:S(2)}) %collective-permute-start.35) | collective-permute-done | bytes 294944 | tf_op jit(solution)/shard_map/ppermute | solution.py:42
  185.8 3.4 %last.1 = (bf16[512,768]{1,0:T(8,128)(2,1)S(1)}, bf16[512,768]{1,0:T(8,128)(2,1)S(1)}, bf16[64,384]{1,0:T(8,128)(2,1)S(1)}, f32[8,128]{1,0:T(8,128)S(1)}) custom-call(f32[512,768]{1,0:T(8,128)S(1)} %get-tuple-element.245.refs_0_, bf16[512,768]{1,0:T(8,128)(2,1)S(1)} %collective-permute-done.33.refs_1_, f32[512,768]{1,0:T(8,128)S(1)} %get-tuple-element.247.refs_2_, ...), custom_call_target="tpu_custom_call" | custom-call | flops 10000000000 | bytes 1000 | tf_op jit(solution)/shard_map/last/pallas_call | solution.py:243
  189.3 10.0 %collective-permute-done.37.refs_2_ = bf16[384,768]{1,0:T(8,128)(2,1)S(1)} collective-permute-done((bf16[384,768]{1,0:T(8,128)(2,1)S(1)}, bf16[384,768]{1,0:T(8,128)(2,1)S(1)}, u32[]{:S(2)}, u32[]{:S(2)}) %collective-permute-start.37) | collective-permute-done | bytes 589856 | tf_op jit(solution)/shard_map/ppermute | solution.py:42
  205.4 7.1 %collective-permute-done.38.refs_2_ = bf16[832,384]{1,0:T(8,128)(2,1)S(1)} collective-permute-done((bf16[832,384]{1,0:T(8,128)(2,1)S(1)}, bf16[832,384]{1,0:T(8,128)(2,1)S(1)}, u32[]{:S(2)}, u32[]{:S(2)}) %collective-permute-start.38) | collective-permute-done | bytes 639008 | tf_op jit(solution)/shard_map/ppermute | solution.py:42
  215.5 11.7 %collective-permute-done.43.refs_3_ = bf16[192,768]{1,0:T(8,128)(2,1)S(1)} collective-permute-done((bf16[192,768]{1,0:T(8,128)(2,1)S(1)}, bf16[192,768]{1,0:T(8,128)(2,1)S(1)}, u32[]{:S(2)}, u32[]{:S(2)}) %collective-permute-start.43) | collective-permute-done | bytes 294944 | tf_op jit(solution)/shard_map/ppermute | solution.py:42
  227.4 5.5 %collective-permute-done.42.refs_3_ = bf16[448,384]{1,0:T(8,128)(2,1)S(1)} collective-permute-done((bf16[448,384]{1,0:T(8,128)(2,1)S(1)}, bf16[448,384]{1,0:T(8,128)(2,1)S(1)}, u32[]{:S(2)}, u32[]{:S(2)}) %collective-permute-start.42) | collective-permute-done | bytes 344096 | tf_op jit(solution)/shard_map/ppermute | solution.py:42
  240.4 4.4 %collective-permute-done.49.refs_2_ = bf16[192,768]{1,0:T(8,128)(2,1)S(1)} collective-permute-done((bf16[192,768]{1,0:T(8,128)(2,1)S(1)}, bf16[192,768]{1,0:T(8,128)(2,1)S(1)}, u32[]{:S(2)}, u32[]{:S(2)}) %collective-permute-start.49) | collective-permute-done | bytes 294944 | tf_op jit(solution)/shard_map/ppermute | solution.py:42
  247.3 7.4 %collective-permute-done.52.refs_3_ = bf16[192,768]{1,0:T(8,128)(2,1)S(1)} collective-permute-done((bf16[192,768]{1,0:T(8,128)(2,1)S(1)}, bf16[192,768]{1,0:T(8,128)(2,1)S(1)}, u32[]{:S(2)}, u32[]{:S(2)}) %collective-permute-start.52) | collective-permute-done | bytes 294944 | tf_op jit(solution)/shard_map/ppermute | solution.py:42
  254.7 3.0 %collect.3 = (f32[2,96,3072]{2,1,0:T(8,128)}, f32[2,384,768]{2,1,0:T(8,128)}, f32[8,128]{1,0:T(8,128)S(1)}) custom-call(bf16[192,768]{1,0:T(8,128)(2,1)S(1)} %get-tuple-element.297.refs_0_, bf16[192,768]{1,0:T(8,128)(2,1)S(1)} %collective-permute-done.51.refs_1_, bf16[192,768]{1,0:T(8,128)(2,1)S(1)} %collective-permute-done.49.refs_2_, ...), custom_call_target="tpu_custom_call" | custom-call | flops 10000000000 | bytes 1000 | tf_op jit(solution)/shard_map/collect/pallas_call | solution.py:243
  263.4 3.4 %collective-permute-done.54.refs_0_ = bf16[256,768]{1,0:T(8,128)(2,1)S(1)} collective-permute-done((bf16[256,768]{1,0:T(8,128)(2,1)S(1)}, bf16[256,768]{1,0:T(8,128)(2,1)S(1)}, u32[]{:S(2)}, u32[]{:S(2)}) %collective-permute-start.54) | collective-permute-done | bytes 393248 | tf_op jit(solution)/shard_map/ppermute | solution.py:42
  (209 shorter events, 87.9 us)
Async XLA Ops:
  7.7 19.8 %collective-permute-start = (bf16[512,768]{1,0:T(8,128)(2,1)}, bf16[512,768]{1,0:T(8,128)(2,1)S(1)}, u32[]{:S(2)}, u32[]{:S(2)}) collective-permute-start(bf16[512,768]{1,0:T(8,128)(2,1)} %get-tuple-element.162), channel_id=1, source_target_pairs={{0,8},{1,9},{2,10},{3,11},{4,12},{5,13},{6,14},{7,15},{8,0},{9,1},... | collective-permute-start | bytes 2359304 | tf_op jit(solution)/shard_map/ppermute | solution.py:42
  11.0 16.5 %collective-permute-start.2 = (bf16[192,384]{1,0:T(8,128)(2,1)S(1)}, bf16[192,384]{1,0:T(8,128)(2,1)S(1)}, u32[]{:S(2)}, u32[]{:S(2)}) collective-permute-start(bf16[192,384]{1,0:T(8,128)(2,1)S(1)} %get-tuple-element.165), channel_id=1, source_target_pairs={{0,2},{1,3},{2,0},{3,1},{4,6},{5,7},{6,4},{7,5},{8,10},{9,11},{10,... | collective-permute-start | bytes 442376 | tf_op jit(solution)/shard_map/ppermute | solution.py:42
  11.6 16.0 %collective-permute-start.3 = (bf16[192,384]{1,0:T(8,128)(2,1)S(1)}, bf16[192,384]{1,0:T(8,128)(2,1)S(1)}, u32[]{:S(2)}, u32[]{:S(2)}) collective-permute-start(bf16[192,384]{1,0:T(8,128)(2,1)S(1)} %get-tuple-element.165), channel_id=1, source_target_pairs={{0,4},{1,5},{2,6},{3,7},{4,0},{5,1},{6,2},{7,3},{8,12},{9,13},{10,... | collective-permute-start | bytes 442376 | tf_op jit(solution)/shard_map/ppermute | solution.py:42
  14.2 13.4 %collective-permute-start.4 = (bf16[192,384]{1,0:T(8,128)(2,1)S(1)}, bf16[192,384]{1,0:T(8,128)(2,1)S(1)}, u32[]{:S(2)}, u32[]{:S(2)}) collective-permute-start(bf16[192,384]{1,0:T(8,128)(2,1)S(1)} %get-tuple-element.165), channel_id=1, source_target_pairs={{0,6},{1,7},{2,4},{3,5},{4,2},{5,3},{6,0},{7,1},{8,14},{9,15},{10,... | collective-permute-start | bytes 442376 | tf_op jit(solution)/shard_map/ppermute | solution.py:42
  16.5 29.9 %collective-permute-start.10 = (bf16[2,96,768]{2,1,0:T(8,128)(2,1)S(1)}, bf16[2,96,768]{2,1,0:T(8,128)(2,1)S(1)}, u32[]{:S(2)}, u32[]{:S(2)}) collective-permute-start(bf16[2,96,768]{2,1,0:T(8,128)(2,1)S(1)} %get-tuple-element.179), channel_id=1, source_target_pairs={{0,4},{1,5},{2,6},{3,7},{4,0},{5,1},{6,2},{7,3},{8,12},{9,13},{10,... | collective-permute-start | bytes 884744 | tf_op jit(solution)/shard_map/ppermute | solution.py:42
  27.7 13.8 %collective-permute-start.6 = (bf16[3,192,384]{2,1,0:T(8,128)(2,1)S(1)}, bf16[3,192,384]{2,1,0:T(8,128)(2,1)S(1)}, u32[]{:S(2)}, u32[]{:S(2)}) collective-permute-start(bf16[3,192,384]{2,1,0:T(8,128)(2,1)S(1)} %get-tuple-element.175.refs_5_), channel_id=1, source_target_pairs={{0,8},{1,17},{2,10},{3,19},{4,12},{5,21},{6,14},{7,23},{8,0},{9,25... | collective-permute-start | bytes 1327112 | tf_op jit(solution)/shard_map/ppermute | solution.py:42
  34.3 12.0 %collective-permute-start.11 = (bf16[2,96,768]{2,1,0:T(8,128)(2,1)S(1)}, bf16[2,96,768]{2,1,0:T(8,128)(2,1)S(1)}, u32[]{:S(2)}, u32[]{:S(2)}) collective-permute-start(bf16[2,96,768]{2,1,0:T(8,128)(2,1)S(1)} %get-tuple-element.181.refs_0_), channel_id=1, source_target_pairs={{0,2},{1,3},{2,0},{3,1},{4,6},{5,7},{6,4},{7,5},{8,10},{9,11},{10,... | collective-permute-start | bytes 884744 | tf_op jit(solution)/shard_map/ppermute | solution.py:42
  46.4 12.8 %collective-permute-start.12 = (bf16[3,96,768]{2,1,0:T(8,128)(2,1)S(1)}, bf16[3,96,768]{2,1,0:T(8,128)(2,1)S(1)}, u32[]{:S(2)}, u32[]{:S(2)}) collective-permute-start(bf16[3,96,768]{2,1,0:T(8,128)(2,1)S(1)} %get-tuple-element.185.refs_2_), channel_id=1, source_target_pairs={{0,8},{1,17},{2,10},{3,19},{4,12},{5,21},{6,14},{7,23},{8,0},{9,25... | collective-permute-start | bytes 1327112 | tf_op jit(solution)/shard_map/ppermute | solution.py:42
  47.5 11.8 %collective-permute-start.13 = (bf16[3,96,768]{2,1,0:T(8,128)(2,1)S(1)}, bf16[3,96,768]{2,1,0:T(8,128)(2,1)S(1)}, u32[]{:S(2)}, u32[]{:S(2)}) collective-permute-start(bf16[3,96,768]{2,1,0:T(8,128)(2,1)S(1)} %get-tuple-element.185.refs_2_), channel_id=1, source_target_pairs={{0,16},{1,9},{2,18},{3,11},{4,20},{5,13},{6,22},{7,15},{8,24},{9,1... | collective-permute-start | bytes 1327112 | tf_op jit(solution)/shard_map/ppermute | solution.py:42
  49.1 16.1 %collective-permute-start.15 = (bf16[2,192,384]{2,1,0:T(8,128)(2,1)S(1)}, bf16[2,192,384]{2,1,0:T(8,128)(2,1)S(1)}, u32[]{:S(2)}, u32[]{:S(2)}) collective-permute-start(bf16[2,192,384]{2,1,0:T(8,128)(2,1)S(1)} %get-tuple-element.189.refs_0_), channel_id=1, source_target_pairs={{0,4},{1,5},{2,6},{3,7},{4,0},{5,1},{6,2},{7,3},{8,12},{9,13},{10,... | collective-permute-start | bytes 884744 | tf_op jit(solution)/shard_map/ppermute | solution.py:42
  65.2 12.2 %collective-permute-start.18 = (bf16[3,192,384]{2,1,0:T(8,128)(2,1)S(1)}, bf16[3,192,384]{2,1,0:T(8,128)(2,1)S(1)}, u32[]{:S(2)}, u32[]{:S(2)}) collective-permute-start(bf16[3,192,384]{2,1,0:T(8,128)(2,1)S(1)} %get-tuple-element.197.refs_5_), channel_id=1, source_target_pairs={{0,8},{1,17},{2,10},{3,19},{4,12},{5,21},{6,14},{7,23},{8,0},{9,25... | collective-permute-start | bytes 1327112 | tf_op jit(solution)/shard_map/ppermute | solution.py:42
  67.5 13.9 %collective-permute-start.17 = (bf16[2,96,768]{2,1,0:T(8,128)(2,1)S(1)}, bf16[2,96,768]{2,1,0:T(8,128)(2,1)S(1)}, u32[]{:S(2)}, u32[]{:S(2)}) collective-permute-start(bf16[2,96,768]{2,1,0:T(8,128)(2,1)S(1)} %get-tuple-element.198.refs_0_), channel_id=1, source_target_pairs={{0,4},{1,5},{2,6},{3,7},{4,0},{5,1},{6,2},{7,3},{8,12},{9,13},{10,... | collective-permute-start | bytes 884744 | tf_op jit(solution)/shard_map/ppermute | solution.py:42
  81.4 16.9 %collective-permute-start.22 = (bf16[3,96,768]{2,1,0:T(8,128)(2,1)S(1)}, bf16[3,96,768]{2,1,0:T(8,128)(2,1)S(1)}, u32[]{:S(2)}, u32[]{:S(2)}) collective-permute-start(bf16[3,96,768]{2,1,0:T(8,128)(2,1)S(1)} %get-tuple-element.206.refs_2_), channel_id=1, source_target_pairs={{0,8},{1,17},{2,10},{3,19},{4,12},{5,21},{6,14},{7,23},{8,0},{9,25... | collective-permute-start | bytes 1327112 | tf_op jit(solution)/shard_map/ppermute | solution.py:42
  82.5 15.9 %collective-permute-start.23 = (bf16[3,96,768]{2,1,0:T(8,128)(2,1)S(1)}, bf16[3,96,768]{2,1,0:T(8,128)(2,1)S(1)}, u32[]{:S(2)}, u32[]{:S(2)}) collective-permute-start(bf16[3,96,768]{2,1,0:T(8,128)(2,1)S(1)} %get-tuple-element.206.refs_2_), channel_id=1, source_target_pairs={{0,16},{1,9},{2,18},{3,11},{4,20},{5,13},{6,22},{7,15},{8,24},{9,1... | collective-permute-start | bytes 1327112 | tf_op jit(solution)/shard_map/ppermute | solution.py:42
  84.0 14.3 %collective-permute-start.21 = (bf16[3,192,384]{2,1,0:T(8,128)(2,1)S(1)}, bf16[3,192,384]{2,1,0:T(8,128)(2,1)S(1)}, u32[]{:S(2)}, u32[]{:S(2)}) collective-permute-start(bf16[3,192,384]{2,1,0:T(8,128)(2,1)S(1)} %collective-permute-done.18.refs_6_), channel_id=1, source_target_pairs={{0,16},{1,9},{2,18},{3,11},{4,20},{5,13},{6,22},{7,15},{8,24},{9,1... | collective-permute-start | bytes 1327112 | tf_op jit(solution)/shard_map/ppermute | solution.py:42
  122.6 16.3 %collective-permute-start.28 = (bf16[2,4,96,768]{3,2,1,0:T(8,128)(2,1)S(1)}, bf16[2,4,96,768]{3,2,1,0:T(8,128)(2,1)S(1)}, u32[]{:S(2)}, u32[]{:S(2)}) collective-permute-start(bf16[2,4,96,768]{3,2,1,0:T(8,128)(2,1)S(1)} %get-tuple-element.228), channel_id=1, source_target_pairs={{0,8},{1,17},{2,10},{3,19},{4,12},{5,21},{6,14},{7,23},{8,0},{9,25... | collective-permute-start | bytes 3538952 | tf_op jit(solution)/shard_map/ppermute | solution.py:42
  132.0 23.2 %collective-permute-start.31 = (bf16[2,4,192,384]{3,2,1,0:T(8,128)(2,1)S(1)}, bf16[2,4,192,384]{3,2,1,0:T(8,128)(2,1)S(1)}, u32[]{:S(2)}, u32[]{:S(2)}) collective-permute-start(bf16[2,4,192,384]{3,2,1,0:T(8,128)(2,1)S(1)} %get-tuple-element.238), channel_id=1, source_target_pairs={{0,8},{1,17},{2,10},{3,19},{4,12},{5,21},{6,14},{7,23},{8,0},{9,25... | collective-permute-start | bytes 3538952 | tf_op jit(solution)/shard_map/ppermute | solution.py:42
  144.4 11.9 %collective-permute-start.29 = (bf16[512,768]{1,0:T(8,128)(2,1)S(1)}, bf16[512,768]{1,0:T(8,128)(2,1)S(1)}, u32[]{:S(2)}, u32[]{:S(2)}) collective-permute-start(bf16[512,768]{1,0:T(8,128)(2,1)S(1)} %get-tuple-element.230.refs_1_.refs_0_), channel_id=1, source_target_pairs={{0,1},{1,0},{2,3},{3,2},{4,5},{5,4},{6,7},{7,6},{8,9},{9,8},{10,11... | collective-permute-start | bytes 2359304 | tf_op jit(solution)/shard_map/ppermute | solution.py:42
  144.7 15.4 %collective-permute-start.30 = (bf16[384,768]{1,0:T(8,128)(2,1)S(1)}, bf16[384,768]{1,0:T(8,128)(2,1)S(1)}, u32[]{:S(2)}, u32[]{:S(2)}) collective-permute-start(bf16[384,768]{1,0:T(8,128)(2,1)S(1)} %get-tuple-element.236), channel_id=1, source_target_pairs={{0,16},{1,9},{2,18},{3,11},{4,20},{5,13},{6,22},{7,15},{8,24},{9,1... | collective-permute-start | bytes 1769480 | tf_op jit(solution)/shard_map/ppermute | solution.py:42
  165.3 15.2 %collective-permute-start.35 = (bf16[192,768]{1,0:T(8,128)(2,1)S(1)}, bf16[192,768]{1,0:T(8,128)(2,1)S(1)}, u32[]{:S(2)}, u32[]{:S(2)}) collective-permute-start(bf16[192,768]{1,0:T(8,128)(2,1)S(1)} %get-tuple-element.257), channel_id=1, source_target_pairs={{0,4},{1,5},{2,6},{3,7},{4,0},{5,1},{6,2},{7,3},{8,12},{9,13},{10,... | collective-permute-start | bytes 884744 | tf_op jit(solution)/shard_map/ppermute | solution.py:42
  166.6 16.2 %collective-permute-start.34 = (bf16[2,4,96,768]{3,2,1,0:T(8,128)(2,1)S(1)}, bf16[2,4,96,768]{3,2,1,0:T(8,128)(2,1)S(1)}, u32[]{:S(2)}, u32[]{:S(2)}) collective-permute-start(bf16[2,4,96,768]{3,2,1,0:T(8,128)(2,1)S(1)} %get-tuple-element.256), channel_id=1, source_target_pairs={{0,8},{1,17},{2,10},{3,19},{4,12},{5,21},{6,14},{7,23},{8,0},{9,25... | collective-permute-start | bytes 3538952 | tf_op jit(solution)/shard_map/ppermute | solution.py:42
  176.8 25.0 %collective-permute-start.36 = (bf16[2,4,192,384]{3,2,1,0:T(8,128)(2,1)S(1)}, bf16[2,4,192,384]{3,2,1,0:T(8,128)(2,1)S(1)}, u32[]{:S(2)}, u32[]{:S(2)}) collective-permute-start(bf16[2,4,192,384]{3,2,1,0:T(8,128)(2,1)S(1)} %get-tuple-element.265), channel_id=1, source_target_pairs={{0,8},{1,17},{2,10},{3,19},{4,12},{5,21},{6,14},{7,23},{8,0},{9,25... | collective-permute-start | bytes 3538952 | tf_op jit(solution)/shard_map/ppermute | solution.py:42
  180.6 21.9 %collective-permute-start.40 = (bf16[96,768]{1,0:T(8,128)(2,1)S(1)}, bf16[96,768]{1,0:T(8,128)(2,1)S(1)}, u32[]{:S(2)}, u32[]{:S(2)}) collective-permute-start(bf16[96,768]{1,0:T(8,128)(2,1)S(1)} %get-tuple-element.272), channel_id=1, source_target_pairs={{0,2},{1,3},{2,0},{3,1},{4,6},{5,7},{6,4},{7,5},{8,10},{9,11},{10,... | collective-permute-start | bytes 442376 | tf_op jit(solution)/shard_map/ppermute | solution.py:42
  183.0 16.3 %collective-permute-start.37 = (bf16[384,768]{1,0:T(8,128)(2,1)S(1)}, bf16[384,768]{1,0:T(8,128)(2,1)S(1)}, u32[]{:S(2)}, u32[]{:S(2)}) collective-permute-start(bf16[384,768]{1,0:T(8,128)(2,1)S(1)} %get-tuple-element.267), channel_id=1, source_target_pairs={{0,16},{1,9},{2,18},{3,11},{4,20},{5,13},{6,22},{7,15},{8,24},{9,1... | collective-permute-start | bytes 1769480 | tf_op jit(solution)/shard_map/ppermute | solution.py:42
  183.7 18.9 %collective-permute-start.39 = (bf16[384,384]{1,0:T(8,128)(2,1)S(1)}, bf16[384,384]{1,0:T(8,128)(2,1)S(1)}, u32[]{:S(2)}, u32[]{:S(2)}) collective-permute-start(bf16[384,384]{1,0:T(8,128)(2,1)S(1)} %get-tuple-element.271), channel_id=1, source_target_pairs={{0,4},{1,5},{2,6},{3,7},{4,0},{5,1},{6,2},{7,3},{8,12},{9,13},{10,... | collective-permute-start | bytes 884744 | tf_op jit(solution)/shard_map/ppermute | solution.py:42
  202.7 12.6 %collective-permute-start.44 = (bf16[192,384]{1,0:T(8,128)(2,1)S(1)}, bf16[192,384]{1,0:T(8,128)(2,1)S(1)}, u32[]{:S(2)}, u32[]{:S(2)}) collective-permute-start(bf16[192,384]{1,0:T(8,128)(2,1)S(1)} %get-tuple-element.280), channel_id=1, source_target_pairs={{0,2},{1,3},{2,0},{3,1},{4,6},{5,7},{6,4},{7,5},{8,10},{9,11},{10,... | collective-permute-start | bytes 442376 | tf_op jit(solution)/shard_map/ppermute | solution.py:42
  205.1 22.2 %collective-permute-start.43 = (bf16[192,768]{1,0:T(8,128)(2,1)S(1)}, bf16[192,768]{1,0:T(8,128)(2,1)S(1)}, u32[]{:S(2)}, u32[]{:S(2)}) collective-permute-start(bf16[192,768]{1,0:T(8,128)(2,1)S(1)} %get-tuple-element.279), channel_id=1, source_target_pairs={{0,4},{1,5},{2,6},{3,7},{4,0},{5,1},{6,2},{7,3},{8,12},{9,13},{10,... | collective-permute-start | bytes 884744 | tf_op jit(solution)/shard_map/ppermute | solution.py:42
  212.6 20.4 %collective-permute-start.42 = (bf16[448,384]{1,0:T(8,128)(2,1)S(1)}, bf16[448,384]{1,0:T(8,128)(2,1)S(1)}, u32[]{:S(2)}, u32[]{:S(2)}) collective-permute-start(bf16[448,384]{1,0:T(8,128)(2,1)S(1)} %get-tuple-element.278.refs_4_), channel_id=1, source_target_pairs={{0,4},{1,5},{2,6},{3,7},{4,0},{5,1},{6,2},{7,3},{8,12},{9,13},{10,... | collective-permute-start | bytes 1032200 | tf_op jit(solution)/shard_map/ppermute | solution.py:42
  214.4 18.8 %collective-permute-start.41 = (bf16[512,768]{1,0:T(8,128)(2,1)S(1)}, bf16[512,768]{1,0:T(8,128)(2,1)S(1)}, u32[]{:S(2)}, u32[]{:S(2)}) collective-permute-start(bf16[512,768]{1,0:T(8,128)(2,1)S(1)} %get-tuple-element.277), channel_id=1, source_target_pairs={{0,8},{1,9},{2,10},{3,11},{4,12},{5,13},{6,14},{7,15},{8,0},{9,1},... | collective-permute-start | bytes 2359304 | tf_op jit(solution)/shard_map/ppermute | solution.py:42
  215.5 19.6 %collective-permute-start.47 = (bf16[96,384]{1,0:T(8,128)(2,1)S(1)}, bf16[96,384]{1,0:T(8,128)(2,1)S(1)}, u32[]{:S(2)}, u32[]{:S(2)}) collective-permute-start(bf16[96,384]{1,0:T(8,128)(2,1)S(1)} %get-tuple-element.288), channel_id=1, source_target_pairs={{0,1},{1,0},{2,3},{3,2},{4,5},{5,4},{6,7},{7,6},{8,9},{9,8},{10,11... | collective-permute-start | bytes 221192 | tf_op jit(solution)/shard_map/ppermute | solution.py:42
  245.5 12.2 %collective-permute-start.50 = (bf16[256,768]{1,0:T(8,128)(2,1)S(1)}, bf16[256,768]{1,0:T(8,128)(2,1)S(1)}, u32[]{:S(2)}, u32[]{:S(2)}) collective-permute-start(bf16[256,768]{1,0:T(8,128)(2,1)S(1)} %get-tuple-element.299.refs_0_), channel_id=1, source_target_pairs={{0,8},{1,17},{2,10},{3,19},{4,12},{5,21},{6,14},{7,23},{8,0},{9,25... | collective-permute-start | bytes 1179656 | tf_op jit(solution)/shard_map/ppermute | solution.py:42
  246.0 12.9 %collective-permute-start.53 = (bf16[256,768]{1,0:T(8,128)(2,1)S(1)}, bf16[256,768]{1,0:T(8,128)(2,1)S(1)}, u32[]{:S(2)}, u32[]{:S(2)}) collective-permute-start(bf16[256,768]{1,0:T(8,128)(2,1)S(1)} %get-tuple-element.299.refs_0_), channel_id=1, source_target_pairs={{0,16},{1,9},{2,18},{3,11},{4,20},{5,13},{6,22},{7,15},{8,24},{9,1... | collective-permute-start | bytes 1179656 | tf_op jit(solution)/shard_map/ppermute | solution.py:42
  (52 other events, 510.3 us)
where the time goes:
time: 273 us; the launch traced here: 269 us
  waiting for transfers between devices  123 us (45%)
  Pallas kernels  76.2 us (28%)
  starting transfers between devices  61.4 us (22%)
  local copies, waits for them, and re-layouts  5.61 us (2%)
    ppermute x55, waiting for transfers between devices, permute(): return lax.ppermute(value, AXES, pairs)  123 us
    pallas_call x52, Pallas kernels, call(): *made, Order.token = build(max(counts[-1], 1))(*arrays)  76.2 us
    ppermute x55, starting transfers between devices, permute(): return lax.ppermute(value, AXES, pairs)  61.4 us
  transfers between devices with their start and end apart: 55, of which 27 were waited for; matrix products, arithmetic and copies ran while one was open for 1% of the time, Pallas kernels for 23%

commit v1 on v0

--- a/solution.py
+++ b/solution.py
@@ -13,7 +13,8 @@
 F32 = jnp.float32
 BF16 = jnp.bfloat16
 BLOCKS = 4
-FORWARD_COST, BACKWARD_COST = 10**10, 10**10
+EVENT_COST, SHORT_COST = 10**10, 10**9
+FAR_MARK_COST, NEAR_MARK_COST, MIDDLE_COST = 2000000000, 4000000000, 100000000
 ROW_STEP = 256
 
 VMEM = pl.BlockSpec(memory_space=pltpu.VMEM)
@@ -170,25 +171,23 @@
 
 class Order:
     token = None
-    cost = FORWARD_COST
 
     @classmethod
     def begin(cls):
         cls.token = jnp.zeros((8, 128), F32)
-        cls.cost = FORWARD_COST
 
     @classmethod
     def wait(cls, *arrays):
         cls.token = tie(cls.token, *arrays)
 
     @classmethod
-    def mark(cls, *arrays):
+    def mark(cls, *arrays, cost=EVENT_COST):
         cls.wait(*arrays)
-        call(lambda *refs: None, [], [], [], "mark")
+        call(lambda *refs: None, [], [], [], "mark", cost=cost)
         return cls.token
 
 
-def call(kernel, ins, outs, scratch, name, aliases=None, spare=4 * 2**20):
+def call(kernel, ins, outs, scratch, name, aliases=None, spare=4 * 2**20, cost=EVENT_COST):
     buffers = []
     n_ins, n_outs, n_scratch = len(ins), len(outs), len(scratch)
     counts = []
@@ -233,7 +232,7 @@
             + buffers
             + [pltpu.SemaphoreType.DMA((sems,))],
             compiler_params=pltpu.CompilerParams(vmem_limit_bytes=needed + spare),
-            cost_estimate=pl.CostEstimate(flops=Order.cost, bytes_accessed=1000, transcendentals=0),
+            cost_estimate=pl.CostEstimate(flops=cost, bytes_accessed=1000, transcendentals=0),
             input_output_aliases=aliases or {},
             name=name,
         )
@@ -242,6 +241,10 @@
     jax.eval_shape(build(96), *arrays)
     *made, Order.token = build(max(counts[-1], 1))(*arrays)
     return made
+
+
+def plain(*arrays):
+    return [(HBM, array) for array in arrays]
 
 
 def move(name, terms, unit, outs, targets, extra=None):
@@ -347,33 +350,32 @@
         self.place, self.name, self.by_rows = place, name, by_rows
         self.w, self.other_rows, self.layer = w, other_rows, layer
 
-    def join(self, halves, out_piece=None):
+    def join(self, halves, out_pieces=()):
         layer, rows, width = self.layer, self.w.shape[1], self.w.shape[2] // (2 * BLOCKS)
-        beside = out_piece is not None
-        shape = (2, rows, 2 * width) if beside else (2 * rows, width)
+        beside = len(out_pieces) > 0
+        shape = (1 + len(out_pieces), rows, 2 * width) if beside else (2 * rows, width)
 
         def run(w, other, *refs):
-            out_ref, (out, held, copies) = refs[:-3], refs[-3:]
+            out_refs, (out, copies) = refs[:-2], refs[-2:]
             spot = Spot()
             own = w.at[layer, :, rows_at((2 * spot.section + spot.core) * width, width)]
             other = other.at[layer, :, rows_at(spot.section * width, width)]
             arriving = []
             for source, core in ((own, spot.core), (other, 1 - spot.core)):
-                target = held.at[rows_at(core * rows, rows)]
+                target = out.at[rows_at(core * rows, rows)]
                 if beside:
-                    target = held.at[0, :, rows_at(core * width, width)]
+                    target = out.at[0, :, rows_at(core * width, width)]
                 arriving.append(copies.start(source, target))
-            if beside:
-                arriving.append(copies.start(out_ref[0], held.at[1]))
+            for i, ref in enumerate(out_refs):
+                arriving.append(copies.start(ref, out.at[1 + i]))
             for copy in arriving:
                 copy.wait()
-            return [copies.start(held, out)]
 
         (piece,) = call(
             run,
-            [(HBM, self.w), (HBM, halves)] + ([(HBM, out_piece)] if beside else []),
-            [(HBM, shape, BF16)],
-            [(shape, BF16)],
+            plain(self.w, halves, *out_pieces),
+            [(VMEM, shape, BF16)],
+            [],
             "piece_" + self.name,
         )
         return piece
@@ -395,17 +397,18 @@
 
 
 def pairs(own, moved):
-    _, rows, width = own.shape
-
-    def run(own, moved, pair_in, pair_out, copies):
+    n, rows, width = own.shape
+
+    def run(own, moved, pair_in, *refs):
         for i, ref in enumerate((own, moved)):
             for core in range(2):
                 half = pl.ds(core * (width // 2), width // 2)
                 pair_in[i, pl.ds(core * rows, rows)] = ref[0, :, half]
-            pair_out[i] = ref[1]
-
-    shapes = [((2, 2 * rows, width // 2), BF16), ((2, rows, width), BF16)]
-    return call(run, [(VMEM, own), (VMEM, moved)], [(VMEM,) + s for s in shapes], [], "pairs")
+            for j in range(n - 1):
+                refs[j][i] = ref[1 + j]
+
+    shapes = [(VMEM, (2, 2 * rows, width // 2), BF16)] + [(VMEM, (2, rows, width), BF16)] * (n - 1)
+    return call(run, [(VMEM, own), (VMEM, moved)], shapes, [], "pairs")
 
 
 def load_in(layer, sources, scratch, copies):
@@ -962,9 +965,6 @@
 
     def late(*arrays):
         return [(LATE, array) for array in arrays]
-
-    def plain(*arrays):
-        return [(HBM, array) for array in arrays]
 
     def param(array, layer):
         return (VMEM, array[layer][None])
@@ -997,14 +997,13 @@
         other_rows = place.swap_core(for_other)
         received = place.swap_layer(given)
         in_zero.other_rows = in_one.other_rows = other_rows
-        out_zero_moved = place.along_z(out_zero_piece, 1)
         in_zero.shift(in_zero.join(other_rows))
-        pieces_one = in_one.join(other_rows, out_one_piece)
-        out_zero_pair = pack("pair_out0", [out_zero_piece, out_zero_moved])
-        out_zero.moved = [out_zero_moved, place.along_z(out_zero_pair, 2)]
+        own_pieces = in_one.join(other_rows, (out_zero_piece, out_one_piece))
+        moved_pieces = place.along_z(own_pieces, 1)
         Order.wait(received)
         in_zero.one()
-        moved_one = place.along_z(tie(pieces_one, Order.token), 1)
+        pair_in, pair_zero, pair_one = pairs(own_pieces, moved_pieces)
+        out_zero.moved = [(pair_zero, 1, 1), place.along_z(pair_zero, 2)]
     else:
         received = place.swap_layer(given)
         for layer in range(layers):
@@ -1053,15 +1052,14 @@
             mark = Order.mark(in_zero.from_one, in_zero.from_two)
             in_zero.two(mark)
             other_normed = place.swap_core(tie(normed, mark))
-            pair_in, pair_out = pairs(pieces_one, moved_one)
             out_zero.one()
-            in_one.moved = [(pair_in, 1, 1), place.along_z(pair_in, 2)]
+            in_one.moved = [(pair_in, 1, 1), place.along_z(tie(pair_in, out_zero.along), 2)]
             sources_in[0] = in_zero.sources()
         else:
             other_normed = place.swap_core(normed)
         if by_permutes and layer == 1:
-            Order.mark(in_one.far)
-            mark = Order.mark(out_one.from_one, out_one.from_two)
+            Order.mark(in_one.far, cost=FAR_MARK_COST)
+            mark = Order.mark(out_one.from_one, out_one.from_two, cost=NEAR_MARK_COST)
             out_one.two(mark)
             sources_in[1] = in_one.sources()
         hidden, slope, whole_in = call(
@@ -1077,7 +1075,7 @@
             mark = Order.mark(out_zero.from_one, out_zero.from_two)
             out_zero.two(mark)
             in_one.one()
-            out_one.moved = [(pair_out, 1, 1), place.along_z(tie(pair_out, in_one.along), 2)]
+            out_one.moved = [(pair_one, 1, 1), place.along_z(tie(pair_one, mark), 2)]
             sources_out[0] = out_zero.sources()
         if by_permutes and layer == 1:
             sources_out[1] = out_one.sources()
@@ -1106,11 +1104,11 @@
                 [(EARLY, block, F32), column] + mix_outs,
                 [(block, BF16), (block, BF16), (block, BF16)],
                 "middle",
+                cost=MIDDLE_COST,
             )
             kept += [unit_two, inverse_two]
         saved.append(kept)
 
-    Order.cost = BACKWARD_COST
     out_rows, d_second, branch_grad, sums_two = call(
         turn_kernel,
         common + plain(boundary, received),

time: 273 us -> 269 us (0.985)
  starting transfers between devices: 61.4 us -> 58.2 us
    ppermute x55 -> x54, starting transfers between devices: 61.4 us -> 58.2 us  [permute(): return lax.ppermute(value, AXES, pairs)]
    ppermute x55 -> x54, waiting for transfers between devices: 123 us -> 124 us  [permute(): return lax.ppermute(value, AXES, pairs)]
    pallas_call x52 -> x51, Pallas kernels: 76.2 us -> 76 us  [call(): *made, Order.token = build(max(counts[-1], 1))(*arrays)]
  transfers between devices with their start and end apart: 55 -> 54, of which waited for: 27 -> 29; matrix products, arithmetic and copies ran while one was open for 1% -> 1% of each run, Pallas kernels for 23% -> 23%
where the time goes in v1:
time: 269 us; the launch traced here: 265 us
  waiting for transfers between devices  124 us (46%)
  Pallas kernels  76 us (28%)
  starting transfers between devices  58.2 us (22%)
  local copies, waits for them, and re-layouts  3.91 us (1%)
    ppermute x54, waiting for transfers between devices, permute(): return lax.ppermute(value, AXES, pairs)  124 us
    pallas_call x51, Pallas kernels, call(): *made, Order.token = build(max(counts[-1], 1))(*arrays)  76 us
    ppermute x54, starting transfers between devices, permute(): return lax.ppermute(value, AXES, pairs)  58.2 us
  transfers between devices with their start and end apart: 54, of which 29 were waited for; matrix products, arithmetic and copies ran while one was open for 1% of the time, Pallas kernels for 23%

profile of v1, /device:TPU:0, one launch (start us, length us, event | category | flops | bytes accessed | tf_op | source)
XLA Modules:
  0.0 264.5 jit_solution(5833822022474562388)
XLA Ops:
  1.3 3.3 %prepare.1 = (bf16[512,768]{1,0:T(8,128)(2,1)}, bf16[2,96,1536]{2,1,0:T(8,128)(2,1)}, bf16[96,768]{1,0:T(8,128)(2,1)}, bf16[96,768]{1,0:T(8,128)(2,1)}, f32[8,128]{1,0:T(8,128)}) custom-call(bf16[1,1024,768]{2,1,0:T(8,128)(2,1)} %refs_8_.2, bf16[2,96,3072]{2,1,0:T(8,128)(2,1)} %refs_3_.4, bf16[2,384,768]{2,1,0:T(8,128)(2,1)} %refs_1_.7, ...), custom_call_target="tpu_custom_call" | custom-call | flops 10000000000 | bytes 1000 | tf_op jit(solution)/shard_map/prepare/pallas_call | solution.py:242
  14.9 11.1 %collective-permute-done.refs_2_.refs_9_ = bf16[512,768]{1,0:T(8,128)(2,1)S(1)} collective-permute-done((bf16[512,768]{1,0:T(8,128)(2,1)}, bf16[512,768]{1,0:T(8,128)(2,1)S(1)}, u32[]{:S(2)}, u32[]{:S(2)}) %collective-permute-start) | collective-permute-done | bytes 786464 | tf_op jit(solution)/shard_map/ppermute | solution.py:43
  33.9 3.4 %first_mix.1 = (bf16[512,512]{1,0:T(8,128)(2,1)S(1)}, bf16[512,512]{1,0:T(8,128)(2,1)S(1)}, f32[512,768]{1,0:T(8,128)S(1)}, f32[512,1]{1,0:T(8,128)S(1)}, bf16[5...) custom-call(s32[16]{0:T(128)S(1)} %select_n.89.refs_0_, bf16[1,1024,768]{2,1,0:T(8,128)(2,1)S(1)} %copy-done.6, ...), custom_call_target="tpu_custom_call" | custom-call | flops 10000000000 | bytes 1000 | tf_op jit(solution)/shard_map/first_mix/pallas_call | solution.py:242
  40.7 6.0 %collective-permute-done.10.refs_1_ = bf16[2,96,768]{2,1,0:T(8,128)(2,1)S(1)} collective-permute-done((bf16[2,96,768]{2,1,0:T(8,128)(2,1)S(1)}, bf16[2,96,768]{2,1,0:T(8,128)(2,1)S(1)}, u32[]{:S(2)}, u32[]{:S(2)}) %collective-permute-start.10) | collective-permute-done | bytes 294944 | tf_op jit(solution)/shard_map/ppermute | solution.py:43
  49.5 5.9 %expand.2 = (bf16[2,1024,768]{2,1,0:T(8,128)(2,1)S(1)}, bf16[2,1024,768]{2,1,0:T(8,128)(2,1)S(1)}, bf16[2,768,768]{2,1,0:T(8,128)(2,1)S(1)}, f32[8,128]{1,0:T(8,128)S(1)}) custom-call(bf16[512,768]{1,0:T(8,128)(2,1)S(1)} %get-tuple-element.177.refs_0_.refs_3_, bf16[512,768]{1,0:T(8,128)(2,1)S(1)} %collective-permute-done.8.refs_1_.refs_4_, ...), custom_call_target="tpu_custom_call" | custom-call | flops 10000000000 | bytes 1000 | tf_op jit(solution)/shard_map/expand/pallas_call | solution.py:242
  55.5 3.5 %collective-permute-done.11.refs_3_ = bf16[3,96,768]{2,1,0:T(8,128)(2,1)S(1)} collective-permute-done((bf16[3,96,768]{2,1,0:T(8,128)(2,1)S(1)}, bf16[3,96,768]{2,1,0:T(8,128)(2,1)S(1)}, u32[]{:S(2)}, u32[]{:S(2)}) %collective-permute-start.11) | collective-permute-done | bytes 442400 | tf_op jit(solution)/shard_map/ppermute | solution.py:43
  59.6 4.4 %collective-permute-done.14.refs_1_ = bf16[2,192,384]{2,1,0:T(8,128)(2,1)S(1)} collective-permute-done((bf16[2,192,384]{2,1,0:T(8,128)(2,1)S(1)}, bf16[2,192,384]{2,1,0:T(8,128)(2,1)S(1)}, u32[]{:S(2)}, u32[]{:S(2)}) %collective-permute-start.14) | collective-permute-done | bytes 294944 | tf_op jit(solution)/shard_map/ppermute | solution.py:43
  65.4 4.7 %collective-permute-done.13.refs_5_ = bf16[3,96,768]{2,1,0:T(8,128)(2,1)S(1)} collective-permute-done((bf16[3,96,768]{2,1,0:T(8,128)(2,1)S(1)}, bf16[3,96,768]{2,1,0:T(8,128)(2,1)S(1)}, u32[]{:S(2)}, u32[]{:S(2)}) %collective-permute-start.13) | collective-permute-done | bytes 442400 | tf_op jit(solution)/shard_map/ppermute | solution.py:43
  70.1 5.2 %contract.2 = (f32[512,768]{1,0:T(8,128)S(1)}, bf16[512,768]{1,0:T(8,128)(2,1)S(1)}, bf16[1536,768]{1,0:T(8,128)(2,1)S(1)}, f32[8,128]{1,0:T(8,128)S(1)}) custom-call(bf16[2,1024,768]{2,1,0:T(8,128)(2,1)S(1)} %get-tuple-element.181.refs_0_, bf16[2,384,768]{2,1,0:T(8,128)(2,1)S(1)} %copy-done.8, bf16[3,96,768]{2,1,0:T(8,128)(2,1)S(1)} %get-tuple-element.182.refs_2_, ...), custom_call_target="tpu_custom_call" | custom-call | flops 10000000000 | bytes 1000 | tf_op jit(solution)/shard_map/contract/pallas_call | solution.py:242
  82.3 3.1 %middle.1 = (f32[512,768]{1,0:T(8,128)S(1)}, f32[512,1]{1,0:T(8,128)S(1)}, f32[512,768]{1,0:T(8,128)S(1)}, f32[512,1]{1,0:T(8,128)S(1)}, bf16[512,768]{1,0:T(8,128)(2,1)S(1)}, /*index=5*/f32[8,128]{1,0:T(8,128)S(1)}) custom-call(f32[512,768]{1,0:T(8,128)S(1)} %get-tuple-element.189.refs_0_, bf16[512,768]{1,0:T(8,128)(2,1)S(1)} %collective-permute-done.15.refs_1_, ...), custom_call_target="tpu_custom_call" | custom-call | flops 100000000 | bytes 1000 | tf_op jit(solution)/shard_map/middle/pallas_call | solution.py:242
  85.5 9.7 %collective-permute-done.20.refs_8_ = bf16[3,192,384]{2,1,0:T(8,128)(2,1)S(1)} collective-permute-done((bf16[3,192,384]{2,1,0:T(8,128)(2,1)S(1)}, bf16[3,192,384]{2,1,0:T(8,128)(2,1)S(1)}, u32[]{:S(2)}, u32[]{:S(2)}) %collective-permute-start.20) | collective-permute-done | bytes 442400 | tf_op jit(solution)/shard_map/ppermute | solution.py:43
  96.8 6.2 %expand.3 = (bf16[2,1024,768]{2,1,0:T(8,128)(2,1)S(1)}, bf16[2,1024,768]{2,1,0:T(8,128)(2,1)S(1)}, bf16[2,768,768]{2,1,0:T(8,128)(2,1)S(1)}, f32[8,128]{1,0:T(8,128)S(1)}) custom-call(bf16[512,768]{1,0:T(8,128)(2,1)S(1)} %get-tuple-element.200.refs_0_.refs_3_, bf16[512,768]{1,0:T(8,128)(2,1)S(1)} %collective-permute-done.19.refs_1_.refs_4_, ...), custom_call_target="tpu_custom_call" | custom-call | flops 10000000000 | bytes 1000 | tf_op jit(solution)/shard_map/expand/pallas_call | solution.py:242
  103.6 5.2 %contract.3 = (f32[512,768]{1,0:T(8,128)S(1)}, bf16[512,768]{1,0:T(8,128)(2,1)S(1)}, bf16[1536,768]{1,0:T(8,128)(2,1)S(1)}, f32[8,128]{1,0:T(8,128)S(1)}) custom-call(bf16[2,1024,768]{2,1,0:T(8,128)(2,1)S(1)} %get-tuple-element.206.refs_0_, bf16[2,384,768]{2,1,0:T(8,128)(2,1)S(1)} %copy-done.8, bf16[3,96,768]{2,1,0:T(8,128)(2,1)S(1)} %get-tuple-element.204.refs_2_, ...), custom_call_target="tpu_custom_call" | custom-call | flops 10000000000 | bytes 1000 | tf_op jit(solution)/shard_map/contract/pallas_call | solution.py:242
  120.5 8.2 %shrink.2 = (bf16[2,4,192,384]{3,2,1,0:T(8,128)(2,1)S(1)}, bf16[2,4,192,384]{3,2,1,0:T(8,128)(2,1)S(1)}, f32[1,3072]{1,0:T(1,128)S(1)}, f32[512,768]{1,0:T(8,128...) custom-call(bf16[512,768]{1,0:T(8,128)(2,1)S(1)} %get-tuple-element.213.refs_1_.refs_0_, ...), custom_call_target="tpu_custom_call" | custom-call | flops 10000000000 | bytes 1000 | tf_op jit(solution)/shard_map/shrink/pallas_call | solution.py:242
  130.2 5.4 %collective-permute-done.27.refs_1_ = bf16[2,4,96,768]{3,2,1,0:T(8,128)(2,1)S(1)} collective-permute-done((bf16[2,4,96,768]{3,2,1,0:T(8,128)(2,1)S(1)}, bf16[2,4,96,768]{3,2,1,0:T(8,128)(2,1)S(1)}, u32[]{:S(2)}, u32[]{:S(2)}) %collective-permute-start.27) | collective-permute-done | bytes 1179680 | tf_op jit(solution)/shard_map/ppermute | solution.py:43
  135.6 4.1 %relay.1 = (f32[8,768]{1,0:T(8,128)S(1)}, f32[512,768]{1,0:T(8,128)S(1)}, bf16[512,768]{1,0:T(8,128)(2,1)S(1)}, f32[8,768]{1,0:T(8,128)S(1)}, f32[8,128]{1,0:T(8,128)S(1)}) custom-call(f32[512,768]{1,0:T(8,128)S(1)} %get-tuple-element.219.refs_0_, bf16[512,768]{1,0:T(8,128)(2,1)S(1)} %collective-permute-done.26.refs_1_, ...), custom_call_target="tpu_custom_call" | custom-call | flops 10000000000 | bytes 1000 | tf_op jit(solution)/shard_map/relay/pallas_call | solution.py:242
  141.5 11.8 %collective-permute-done.30.refs_1_ = bf16[2,4,192,384]{3,2,1,0:T(8,128)(2,1)S(1)} collective-permute-done((bf16[2,4,192,384]{3,2,1,0:T(8,128)(2,1)S(1)}, bf16[2,4,192,384]{3,2,1,0:T(8,128)(2,1)S(1)}, u32[]{:S(2)}, u32[]{:S(2)}) %collective-permute-start.30) | collective-permute-done | bytes 1179680 | tf_op jit(solution)/shard_map/ppermute | solution.py:43
  155.1 2.9 %grad_out.3 = (bf16[2,4,96,768]{3,2,1,0:T(8,128)(2,1)S(1)}, bf16[2,4,96,768]{3,2,1,0:T(8,128)(2,1)S(1)}, f32[8,128]{1,0:T(8,128)S(1)}) custom-call(bf16[2,1024,768]{2,1,0:T(8,128)(2,1)S(1)} %copy-done.18, bf16[512,768]{1,0:T(8,128)(2,1)S(1)} %get-tuple-element.228.refs_1_.refs_0_, bf16[512,768]{1,0:T(8,128)(2,1)S(1)} %collective-permute-done.28.refs_2_.refs_1_, ...), custom_call_target="tpu_custom_call" | custom-call | flops 10000000000 | bytes 1000 | tf_op jit(solution)/shard_map/grad_out/pallas_call | solution.py:242
  158.2 5.1 %collective-permute-done.31.refs_2_ = bf16[768,384]{1,0:T(8,128)(2,1)S(1)} collective-permute-done((bf16[768,384]{1,0:T(8,128)(2,1)S(1)}, bf16[768,384]{1,0:T(8,128)(2,1)S(1)}, u32[]{:S(2)}, u32[]{:S(2)}) %collective-permute-start.31) | collective-permute-done | bytes 589856 | tf_op jit(solution)/shard_map/ppermute | solution.py:43
  166.8 8.4 %shrink.3 = (bf16[2,4,192,384]{3,2,1,0:T(8,128)(2,1)S(1)}, bf16[2,4,192,384]{3,2,1,0:T(8,128)(2,1)S(1)}, f32[1,3072]{1,0:T(1,128)S(1)}, f32[512,768]{1,0:T(8,128...) custom-call(bf16[512,768]{1,0:T(8,128)(2,1)S(1)} %get-tuple-element.228.refs_1_.refs_0_, ...), custom_call_target="tpu_custom_call" | custom-call | flops 10000000000 | bytes 1000 | tf_op jit(solution)/shard_map/shrink/pallas_call | solution.py:242
  181.8 3.3 %collective-permute-start.38 = (bf16[384,384]{1,0:T(8,128)(2,1)S(1)}, bf16[384,384]{1,0:T(8,128)(2,1)S(1)}, u32[]{:S(2)}, u32[]{:S(2)}) collective-permute-start(bf16[384,384]{1,0:T(8,128)(2,1)S(1)} %get-tuple-element.269), channel_id=1, source_target_pairs={{0,4},{1,5},{2,6},{3,7},{4,0},{5,1},{6,2},{7,3},{8,12},{9,13},{10,... | collective-permute-start | bytes 884744 | tf_op jit(solution)/shard_map/ppermute | solution.py:43
  185.1 3.3 %last.1 = (bf16[512,768]{1,0:T(8,128)(2,1)S(1)}, bf16[512,768]{1,0:T(8,128)(2,1)S(1)}, bf16[64,384]{1,0:T(8,128)(2,1)S(1)}, f32[8,128]{1,0:T(8,128)S(1)}) custom-call(f32[512,768]{1,0:T(8,128)S(1)} %get-tuple-element.243.refs_0_, bf16[512,768]{1,0:T(8,128)(2,1)S(1)} %collective-permute-done.32.refs_1_, f32[512,768]{1,0:T(8,128)S(1)} %get-tuple-element.245.refs_2_, ...), custom_call_target="tpu_custom_call" | custom-call | flops 10000000000 | bytes 1000 | tf_op jit(solution)/shard_map/last/pallas_call | solution.py:242
  188.4 8.9 %collective-permute-done.36.refs_2_ = bf16[384,768]{1,0:T(8,128)(2,1)S(1)} collective-permute-done((bf16[384,768]{1,0:T(8,128)(2,1)S(1)}, bf16[384,768]{1,0:T(8,128)(2,1)S(1)}, u32[]{:S(2)}, u32[]{:S(2)}) %collective-permute-start.36) | collective-permute-done | bytes 589856 | tf_op jit(solution)/shard_map/ppermute | solution.py:43
  197.4 3.4 %collective-permute-done.35.refs_1_ = bf16[2,4,192,384]{3,2,1,0:T(8,128)(2,1)S(1)} collective-permute-done((bf16[2,4,192,384]{3,2,1,0:T(8,128)(2,1)S(1)}, bf16[2,4,192,384]{3,2,1,0:T(8,128)(2,1)S(1)}, u32[]{:S(2)}, u32[]{:S(2)}) %collective-permute-start.35) | collective-permute-done | bytes 1179680 | tf_op jit(solution)/shard_map/ppermute | solution.py:43
  201.8 5.2 %collective-permute-start.43 = (bf16[192,384]{1,0:T(8,128)(2,1)S(1)}, bf16[192,384]{1,0:T(8,128)(2,1)S(1)}, u32[]{:S(2)}, u32[]{:S(2)}) collective-permute-start(bf16[192,384]{1,0:T(8,128)(2,1)S(1)} %get-tuple-element.278), channel_id=1, source_target_pairs={{0,2},{1,3},{2,0},{3,1},{4,6},{5,7},{6,4},{7,5},{8,10},{9,11},{10,... | collective-permute-start | bytes 442376 | tf_op jit(solution)/shard_map/ppermute | solution.py:43
  207.0 4.5 %collective-permute-done.37.refs_2_ = bf16[832,384]{1,0:T(8,128)(2,1)S(1)} collective-permute-done((bf16[832,384]{1,0:T(8,128)(2,1)S(1)}, bf16[832,384]{1,0:T(8,128)(2,1)S(1)}, u32[]{:S(2)}, u32[]{:S(2)}) %collective-permute-start.37) | collective-permute-done | bytes 639008 | tf_op jit(solution)/shard_map/ppermute | solution.py:43
  215.3 12.6 %collective-permute-done.42.refs_3_ = bf16[192,768]{1,0:T(8,128)(2,1)S(1)} collective-permute-done((bf16[192,768]{1,0:T(8,128)(2,1)S(1)}, bf16[192,768]{1,0:T(8,128)(2,1)S(1)}, u32[]{:S(2)}, u32[]{:S(2)}) %collective-permute-start.42) | collective-permute-done | bytes 294944 | tf_op jit(solution)/shard_map/ppermute | solution.py:43
  228.1 3.8 %collective-permute-done.41.refs_3_ = bf16[448,384]{1,0:T(8,128)(2,1)S(1)} collective-permute-done((bf16[448,384]{1,0:T(8,128)(2,1)S(1)}, bf16[448,384]{1,0:T(8,128)(2,1)S(1)}, u32[]{:S(2)}, u32[]{:S(2)}) %collective-permute-start.41) | collective-permute-done | bytes 344096 | tf_op jit(solution)/shard_map/ppermute | solution.py:43
  238.0 2.9 %collective-permute-done.48.refs_2_ = bf16[192,768]{1,0:T(8,128)(2,1)S(1)} collective-permute-done((bf16[192,768]{1,0:T(8,128)(2,1)S(1)}, bf16[192,768]{1,0:T(8,128)(2,1)S(1)}, u32[]{:S(2)}, u32[]{:S(2)}) %collective-permute-start.48) | collective-permute-done | bytes 294944 | tf_op jit(solution)/shard_map/ppermute | solution.py:43
  246.2 4.0 %collective-permute-done.51.refs_3_ = bf16[192,768]{1,0:T(8,128)(2,1)S(1)} collective-permute-done((bf16[192,768]{1,0:T(8,128)(2,1)S(1)}, bf16[192,768]{1,0:T(8,128)(2,1)S(1)}, u32[]{:S(2)}, u32[]{:S(2)}) %collective-permute-start.51) | collective-permute-done | bytes 294944 | tf_op jit(solution)/shard_map/ppermute | solution.py:43
  250.2 3.0 %collect.3 = (f32[2,96,3072]{2,1,0:T(8,128)}, f32[2,384,768]{2,1,0:T(8,128)}, f32[8,128]{1,0:T(8,128)S(1)}) custom-call(bf16[192,768]{1,0:T(8,128)(2,1)S(1)} %get-tuple-element.295.refs_0_, bf16[192,768]{1,0:T(8,128)(2,1)S(1)} %collective-permute-done.50.refs_1_, bf16[192,768]{1,0:T(8,128)(2,1)S(1)} %collective-permute-done.48.refs_2_, ...), custom_call_target="tpu_custom_call" | custom-call | flops 10000000000 | bytes 1000 | tf_op jit(solution)/shard_map/collect/pallas_call | solution.py:242
  258.8 3.5 %collective-permute-done.53.refs_0_ = bf16[256,768]{1,0:T(8,128)(2,1)S(1)} collective-permute-done((bf16[256,768]{1,0:T(8,128)(2,1)S(1)}, bf16[256,768]{1,0:T(8,128)(2,1)S(1)}, u32[]{:S(2)}, u32[]{:S(2)}) %collective-permute-start.53) | collective-permute-done | bytes 393248 | tf_op jit(solution)/shard_map/ppermute | solution.py:43
  (210 shorter events, 86.7 us)
Async XLA Ops:
  5.1 20.9 %collective-permute-start = (bf16[512,768]{1,0:T(8,128)(2,1)}, bf16[512,768]{1,0:T(8,128)(2,1)S(1)}, u32[]{:S(2)}, u32[]{:S(2)}) collective-permute-start(bf16[512,768]{1,0:T(8,128)(2,1)} %get-tuple-element.161), channel_id=1, source_target_pairs={{0,8},{1,9},{2,10},{3,11},{4,12},{5,13},{6,14},{7,15},{8,0},{9,1},... | collective-permute-start | bytes 2359304 | tf_op jit(solution)/shard_map/ppermute | solution.py:43
  9.3 16.7 %collective-permute-start.3 = (bf16[192,384]{1,0:T(8,128)(2,1)S(1)}, bf16[192,384]{1,0:T(8,128)(2,1)S(1)}, u32[]{:S(2)}, u32[]{:S(2)}) collective-permute-start(bf16[192,384]{1,0:T(8,128)(2,1)S(1)} %get-tuple-element.168), channel_id=1, source_target_pairs={{0,2},{1,3},{2,0},{3,1},{4,6},{5,7},{6,4},{7,5},{8,10},{9,11},{10,... | collective-permute-start | bytes 442376 | tf_op jit(solution)/shard_map/ppermute | solution.py:43
  10.9 15.1 %collective-permute-start.4 = (bf16[192,384]{1,0:T(8,128)(2,1)S(1)}, bf16[192,384]{1,0:T(8,128)(2,1)S(1)}, u32[]{:S(2)}, u32[]{:S(2)}) collective-permute-start(bf16[192,384]{1,0:T(8,128)(2,1)S(1)} %get-tuple-element.168), channel_id=1, source_target_pairs={{0,4},{1,5},{2,6},{3,7},{4,0},{5,1},{6,2},{7,3},{8,12},{9,13},{10,... | collective-permute-start | bytes 442376 | tf_op jit(solution)/shard_map/ppermute | solution.py:43
  13.5 12.5 %collective-permute-start.5 = (bf16[192,384]{1,0:T(8,128)(2,1)S(1)}, bf16[192,384]{1,0:T(8,128)(2,1)S(1)}, u32[]{:S(2)}, u32[]{:S(2)}) collective-permute-start(bf16[192,384]{1,0:T(8,128)(2,1)S(1)} %get-tuple-element.168), channel_id=1, source_target_pairs={{0,6},{1,7},{2,4},{3,5},{4,2},{5,3},{6,0},{7,1},{8,14},{9,15},{10,... | collective-permute-start | bytes 442376 | tf_op jit(solution)/shard_map/ppermute | solution.py:43
  14.2 16.9 %collective-permute-start.2 = (bf16[3,96,768]{2,1,0:T(8,128)(2,1)S(1)}, bf16[3,96,768]{2,1,0:T(8,128)(2,1)S(1)}, u32[]{:S(2)}, u32[]{:S(2)}) collective-permute-start(bf16[3,96,768]{2,1,0:T(8,128)(2,1)S(1)} %get-tuple-element.167.refs_0_), channel_id=1, source_target_pairs={{0,2},{1,3},{2,0},{3,1},{4,6},{5,7},{6,4},{7,5},{8,10},{9,11},{10,... | collective-permute-start | bytes 1327112 | tf_op jit(solution)/shard_map/ppermute | solution.py:43
  26.0 12.9 %collective-permute-start.6 = (bf16[3,192,384]{2,1,0:T(8,128)(2,1)S(1)}, bf16[3,192,384]{2,1,0:T(8,128)(2,1)S(1)}, u32[]{:S(2)}, u32[]{:S(2)}) collective-permute-start(bf16[3,192,384]{2,1,0:T(8,128)(2,1)S(1)} %get-tuple-element.175.refs_5_), channel_id=1, source_target_pairs={{0,8},{1,17},{2,10},{3,19},{4,12},{5,21},{6,14},{7,23},{8,0},{9,25... | collective-permute-start | bytes 1327112 | tf_op jit(solution)/shard_map/ppermute | solution.py:43
  27.9 11.1 %collective-permute-start.7 = (bf16[3,192,384]{2,1,0:T(8,128)(2,1)S(1)}, bf16[3,192,384]{2,1,0:T(8,128)(2,1)S(1)}, u32[]{:S(2)}, u32[]{:S(2)}) collective-permute-start(bf16[3,192,384]{2,1,0:T(8,128)(2,1)S(1)} %get-tuple-element.175.refs_5_), channel_id=1, source_target_pairs={{0,16},{1,9},{2,18},{3,11},{4,20},{5,13},{6,22},{7,15},{8,24},{9,1... | collective-permute-start | bytes 1327112 | tf_op jit(solution)/shard_map/ppermute | solution.py:43
  31.1 15.5 %collective-permute-start.10 = (bf16[2,96,768]{2,1,0:T(8,128)(2,1)S(1)}, bf16[2,96,768]{2,1,0:T(8,128)(2,1)S(1)}, u32[]{:S(2)}, u32[]{:S(2)}) collective-permute-start(bf16[2,96,768]{2,1,0:T(8,128)(2,1)S(1)} %get-tuple-element.179.refs_0_), channel_id=1, source_target_pairs={{0,4},{1,5},{2,6},{3,7},{4,0},{5,1},{6,2},{7,3},{8,12},{9,13},{10,... | collective-permute-start | bytes 884744 | tf_op jit(solution)/shard_map/ppermute | solution.py:43
  46.7 12.3 %collective-permute-start.11 = (bf16[3,96,768]{2,1,0:T(8,128)(2,1)S(1)}, bf16[3,96,768]{2,1,0:T(8,128)(2,1)S(1)}, u32[]{:S(2)}, u32[]{:S(2)}) collective-permute-start(bf16[3,96,768]{2,1,0:T(8,128)(2,1)S(1)} %get-tuple-element.182.refs_2_), channel_id=1, source_target_pairs={{0,8},{1,17},{2,10},{3,19},{4,12},{5,21},{6,14},{7,23},{8,0},{9,25... | collective-permute-start | bytes 1327112 | tf_op jit(solution)/shard_map/ppermute | solution.py:43
  49.5 14.5 %collective-permute-start.14 = (bf16[2,192,384]{2,1,0:T(8,128)(2,1)S(1)}, bf16[2,192,384]{2,1,0:T(8,128)(2,1)S(1)}, u32[]{:S(2)}, u32[]{:S(2)}) collective-permute-start(bf16[2,192,384]{2,1,0:T(8,128)(2,1)S(1)} %get-tuple-element.187.refs_0_), channel_id=1, source_target_pairs={{0,4},{1,5},{2,6},{3,7},{4,0},{5,1},{6,2},{7,3},{8,12},{9,13},{10,... | collective-permute-start | bytes 884744 | tf_op jit(solution)/shard_map/ppermute | solution.py:43
  64.0 11.3 %collective-permute-start.17 = (bf16[3,192,384]{2,1,0:T(8,128)(2,1)S(1)}, bf16[3,192,384]{2,1,0:T(8,128)(2,1)S(1)}, u32[]{:S(2)}, u32[]{:S(2)}) collective-permute-start(bf16[3,192,384]{2,1,0:T(8,128)(2,1)S(1)} %get-tuple-element.197.refs_5_), channel_id=1, source_target_pairs={{0,8},{1,17},{2,10},{3,19},{4,12},{5,21},{6,14},{7,23},{8,0},{9,25... | collective-permute-start | bytes 1327112 | tf_op jit(solution)/shard_map/ppermute | solution.py:43
  64.9 12.0 %collective-permute-start.18 = (bf16[3,192,384]{2,1,0:T(8,128)(2,1)S(1)}, bf16[3,192,384]{2,1,0:T(8,128)(2,1)S(1)}, u32[]{:S(2)}, u32[]{:S(2)}) collective-permute-start(bf16[3,192,384]{2,1,0:T(8,128)(2,1)S(1)} %get-tuple-element.197.refs_5_), channel_id=1, source_target_pairs={{0,16},{1,9},{2,18},{3,11},{4,20},{5,13},{6,22},{7,15},{8,24},{9,1... | collective-permute-start | bytes 1327112 | tf_op jit(solution)/shard_map/ppermute | solution.py:43
  65.4 13.5 %collective-permute-start.16 = (bf16[2,96,768]{2,1,0:T(8,128)(2,1)S(1)}, bf16[2,96,768]{2,1,0:T(8,128)(2,1)S(1)}, u32[]{:S(2)}, u32[]{:S(2)}) collective-permute-start(bf16[2,96,768]{2,1,0:T(8,128)(2,1)S(1)} %get-tuple-element.195.refs_0_), channel_id=1, source_target_pairs={{0,4},{1,5},{2,6},{3,7},{4,0},{5,1},{6,2},{7,3},{8,12},{9,13},{10,... | collective-permute-start | bytes 884744 | tf_op jit(solution)/shard_map/ppermute | solution.py:43
  79.0 16.2 %collective-permute-start.21 = (bf16[3,96,768]{2,1,0:T(8,128)(2,1)S(1)}, bf16[3,96,768]{2,1,0:T(8,128)(2,1)S(1)}, u32[]{:S(2)}, u32[]{:S(2)}) collective-permute-start(bf16[3,96,768]{2,1,0:T(8,128)(2,1)S(1)} %get-tuple-element.204.refs_2_), channel_id=1, source_target_pairs={{0,8},{1,17},{2,10},{3,19},{4,12},{5,21},{6,14},{7,23},{8,0},{9,25... | collective-permute-start | bytes 1327112 | tf_op jit(solution)/shard_map/ppermute | solution.py:43
  80.2 15.0 %collective-permute-start.22 = (bf16[3,96,768]{2,1,0:T(8,128)(2,1)S(1)}, bf16[3,96,768]{2,1,0:T(8,128)(2,1)S(1)}, u32[]{:S(2)}, u32[]{:S(2)}) collective-permute-start(bf16[3,96,768]{2,1,0:T(8,128)(2,1)S(1)} %get-tuple-element.204.refs_2_), channel_id=1, source_target_pairs={{0,16},{1,9},{2,18},{3,11},{4,20},{5,13},{6,22},{7,15},{8,24},{9,1... | collective-permute-start | bytes 1327112 | tf_op jit(solution)/shard_map/ppermute | solution.py:43
  81.8 13.4 %collective-permute-start.20 = (bf16[3,192,384]{2,1,0:T(8,128)(2,1)S(1)}, bf16[3,192,384]{2,1,0:T(8,128)(2,1)S(1)}, u32[]{:S(2)}, u32[]{:S(2)}) collective-permute-start(bf16[3,192,384]{2,1,0:T(8,128)(2,1)S(1)} %collective-permute-done.17.refs_6_), channel_id=1, source_target_pairs={{0,16},{1,9},{2,18},{3,11},{4,20},{5,13},{6,22},{7,15},{8,24},{9,1... | collective-permute-start | bytes 1327112 | tf_op jit(solution)/shard_map/ppermute | solution.py:43
  85.4 11.4 %collective-permute-start.19 = (bf16[512,768]{1,0:T(8,128)(2,1)S(1)}, bf16[512,768]{1,0:T(8,128)(2,1)S(1)}, u32[]{:S(2)}, u32[]{:S(2)}) collective-permute-start(bf16[512,768]{1,0:T(8,128)(2,1)S(1)} %get-tuple-element.200.refs_0_.refs_3_), channel_id=1, source_target_pairs={{0,1},{1,0},{2,3},{3,2},{4,5},{5,4},{6,7},{7,6},{8,9},{9,8},{10,11... | collective-permute-start | bytes 2359304 | tf_op jit(solution)/shard_map/ppermute | solution.py:43
  119.3 16.3 %collective-permute-start.27 = (bf16[2,4,96,768]{3,2,1,0:T(8,128)(2,1)S(1)}, bf16[2,4,96,768]{3,2,1,0:T(8,128)(2,1)S(1)}, u32[]{:S(2)}, u32[]{:S(2)}) collective-permute-start(bf16[2,4,96,768]{3,2,1,0:T(8,128)(2,1)S(1)} %get-tuple-element.226), channel_id=1, source_target_pairs={{0,8},{1,17},{2,10},{3,19},{4,12},{5,21},{6,14},{7,23},{8,0},{9,25... | collective-permute-start | bytes 3538952 | tf_op jit(solution)/shard_map/ppermute | solution.py:43
  129.0 24.3 %collective-permute-start.30 = (bf16[2,4,192,384]{3,2,1,0:T(8,128)(2,1)S(1)}, bf16[2,4,192,384]{3,2,1,0:T(8,128)(2,1)S(1)}, u32[]{:S(2)}, u32[]{:S(2)}) collective-permute-start(bf16[2,4,192,384]{3,2,1,0:T(8,128)(2,1)S(1)} %get-tuple-element.236), channel_id=1, source_target_pairs={{0,8},{1,17},{2,10},{3,19},{4,12},{5,21},{6,14},{7,23},{8,0},{9,25... | collective-permute-start | bytes 3538952 | tf_op jit(solution)/shard_map/ppermute | solution.py:43
  139.7 15.3 %collective-permute-start.28 = (bf16[512,768]{1,0:T(8,128)(2,1)S(1)}, bf16[512,768]{1,0:T(8,128)(2,1)S(1)}, u32[]{:S(2)}, u32[]{:S(2)}) collective-permute-start(bf16[512,768]{1,0:T(8,128)(2,1)S(1)} %get-tuple-element.228.refs_1_.refs_0_), channel_id=1, source_target_pairs={{0,1},{1,0},{2,3},{3,2},{4,5},{5,4},{6,7},{7,6},{8,9},{9,8},{10,11... | collective-permute-start | bytes 2359304 | tf_op jit(solution)/shard_map/ppermute | solution.py:43
  139.9 18.2 %collective-permute-start.29 = (bf16[384,768]{1,0:T(8,128)(2,1)S(1)}, bf16[384,768]{1,0:T(8,128)(2,1)S(1)}, u32[]{:S(2)}, u32[]{:S(2)}) collective-permute-start(bf16[384,768]{1,0:T(8,128)(2,1)S(1)} %get-tuple-element.234), channel_id=1, source_target_pairs={{0,16},{1,9},{2,18},{3,11},{4,20},{5,13},{6,22},{7,15},{8,24},{9,1... | collective-permute-start | bytes 1769480 | tf_op jit(solution)/shard_map/ppermute | solution.py:43
  163.4 13.8 %collective-permute-start.34 = (bf16[192,768]{1,0:T(8,128)(2,1)S(1)}, bf16[192,768]{1,0:T(8,128)(2,1)S(1)}, u32[]{:S(2)}, u32[]{:S(2)}) collective-permute-start(bf16[192,768]{1,0:T(8,128)(2,1)S(1)} %get-tuple-element.255), channel_id=1, source_target_pairs={{0,4},{1,5},{2,6},{3,7},{4,0},{5,1},{6,2},{7,3},{8,12},{9,13},{10,... | collective-permute-start | bytes 884744 | tf_op jit(solution)/shard_map/ppermute | solution.py:43
  164.5 16.5 %collective-permute-start.33 = (bf16[2,4,96,768]{3,2,1,0:T(8,128)(2,1)S(1)}, bf16[2,4,96,768]{3,2,1,0:T(8,128)(2,1)S(1)}, u32[]{:S(2)}, u32[]{:S(2)}) collective-permute-start(bf16[2,4,96,768]{3,2,1,0:T(8,128)(2,1)S(1)} %get-tuple-element.254), channel_id=1, source_target_pairs={{0,8},{1,17},{2,10},{3,19},{4,12},{5,21},{6,14},{7,23},{8,0},{9,25... | collective-permute-start | bytes 3538952 | tf_op jit(solution)/shard_map/ppermute | solution.py:43
  175.3 25.6 %collective-permute-start.35 = (bf16[2,4,192,384]{3,2,1,0:T(8,128)(2,1)S(1)}, bf16[2,4,192,384]{3,2,1,0:T(8,128)(2,1)S(1)}, u32[]{:S(2)}, u32[]{:S(2)}) collective-permute-start(bf16[2,4,192,384]{3,2,1,0:T(8,128)(2,1)S(1)} %get-tuple-element.263), channel_id=1, source_target_pairs={{0,8},{1,17},{2,10},{3,19},{4,12},{5,21},{6,14},{7,23},{8,0},{9,25... | collective-permute-start | bytes 3538952 | tf_op jit(solution)/shard_map/ppermute | solution.py:43
  177.3 24.3 %collective-permute-start.39 = (bf16[96,768]{1,0:T(8,128)(2,1)S(1)}, bf16[96,768]{1,0:T(8,128)(2,1)S(1)}, u32[]{:S(2)}, u32[]{:S(2)}) collective-permute-start(bf16[96,768]{1,0:T(8,128)(2,1)S(1)} %get-tuple-element.270), channel_id=1, source_target_pairs={{0,2},{1,3},{2,0},{3,1},{4,6},{5,7},{6,4},{7,5},{8,10},{9,11},{10,... | collective-permute-start | bytes 442376 | tf_op jit(solution)/shard_map/ppermute | solution.py:43
  181.1 16.2 %collective-permute-start.36 = (bf16[384,768]{1,0:T(8,128)(2,1)S(1)}, bf16[384,768]{1,0:T(8,128)(2,1)S(1)}, u32[]{:S(2)}, u32[]{:S(2)}) collective-permute-start(bf16[384,768]{1,0:T(8,128)(2,1)S(1)} %get-tuple-element.265), channel_id=1, source_target_pairs={{0,16},{1,9},{2,18},{3,11},{4,20},{5,13},{6,22},{7,15},{8,24},{9,1... | collective-permute-start | bytes 1769480 | tf_op jit(solution)/shard_map/ppermute | solution.py:43
  181.8 19.9 %collective-permute-start.38 = (bf16[384,384]{1,0:T(8,128)(2,1)S(1)}, bf16[384,384]{1,0:T(8,128)(2,1)S(1)}, u32[]{:S(2)}, u32[]{:S(2)}) collective-permute-start(bf16[384,384]{1,0:T(8,128)(2,1)S(1)} %get-tuple-element.269), channel_id=1, source_target_pairs={{0,4},{1,5},{2,6},{3,7},{4,0},{5,1},{6,2},{7,3},{8,12},{9,13},{10,... | collective-permute-start | bytes 884744 | tf_op jit(solution)/shard_map/ppermute | solution.py:43
  201.8 13.3 %collective-permute-start.43 = (bf16[192,384]{1,0:T(8,128)(2,1)S(1)}, bf16[192,384]{1,0:T(8,128)(2,1)S(1)}, u32[]{:S(2)}, u32[]{:S(2)}) collective-permute-start(bf16[192,384]{1,0:T(8,128)(2,1)S(1)} %get-tuple-element.278), channel_id=1, source_target_pairs={{0,2},{1,3},{2,0},{3,1},{4,6},{5,7},{6,4},{7,5},{8,10},{9,11},{10,... | collective-permute-start | bytes 442376 | tf_op jit(solution)/shard_map/ppermute | solution.py:43
  207.0 20.9 %collective-permute-start.42 = (bf16[192,768]{1,0:T(8,128)(2,1)S(1)}, bf16[192,768]{1,0:T(8,128)(2,1)S(1)}, u32[]{:S(2)}, u32[]{:S(2)}) collective-permute-start(bf16[192,768]{1,0:T(8,128)(2,1)S(1)} %get-tuple-element.277), channel_id=1, source_target_pairs={{0,4},{1,5},{2,6},{3,7},{4,0},{5,1},{6,2},{7,3},{8,12},{9,13},{10,... | collective-permute-start | bytes 884744 | tf_op jit(solution)/shard_map/ppermute | solution.py:43
  211.6 20.3 %collective-permute-start.41 = (bf16[448,384]{1,0:T(8,128)(2,1)S(1)}, bf16[448,384]{1,0:T(8,128)(2,1)S(1)}, u32[]{:S(2)}, u32[]{:S(2)}) collective-permute-start(bf16[448,384]{1,0:T(8,128)(2,1)S(1)} %get-tuple-element.276.refs_4_), channel_id=1, source_target_pairs={{0,4},{1,5},{2,6},{3,7},{4,0},{5,1},{6,2},{7,3},{8,12},{9,13},{10,... | collective-permute-start | bytes 1032200 | tf_op jit(solution)/shard_map/ppermute | solution.py:43
  213.8 18.3 %collective-permute-start.40 = (bf16[512,768]{1,0:T(8,128)(2,1)S(1)}, bf16[512,768]{1,0:T(8,128)(2,1)S(1)}, u32[]{:S(2)}, u32[]{:S(2)}) collective-permute-start(bf16[512,768]{1,0:T(8,128)(2,1)S(1)} %get-tuple-element.275), channel_id=1, source_target_pairs={{0,8},{1,9},{2,10},{3,11},{4,12},{5,13},{6,14},{7,15},{8,0},{9,1},... | collective-permute-start | bytes 2359304 | tf_op jit(solution)/shard_map/ppermute | solution.py:43
  215.2 18.8 %collective-permute-start.46 = (bf16[96,384]{1,0:T(8,128)(2,1)S(1)}, bf16[96,384]{1,0:T(8,128)(2,1)S(1)}, u32[]{:S(2)}, u32[]{:S(2)}) collective-permute-start(bf16[96,384]{1,0:T(8,128)(2,1)S(1)} %get-tuple-element.286), channel_id=1, source_target_pairs={{0,1},{1,0},{2,3},{3,2},{4,5},{5,4},{6,7},{7,6},{8,9},{9,8},{10,11... | collective-permute-start | bytes 221192 | tf_op jit(solution)/shard_map/ppermute | solution.py:43
  (53 other events, 436.1 us)

commit v2 on v1

--- a/solution.py
+++ b/solution.py
@@ -1263,10 +1263,10 @@
                 aliases={n: 0, n + 1: 1} if started else None,
             )
 
-        Order.wait(rest[2])
-        started = collect(groups[0], zip((3, 0, 2, 1), [mine] + rest), ())
+        Order.mark(rest[2])
         mark = Order.mark(*last_rest)
         far = place.plane_two(tie(last_rest[0], mark))
+        started = collect(groups[0], zip((3, 0, 2, 1), [mine] + rest), ())
         started = collect(groups[1], zip((3, 0, 2), [last_mine] + last_rest), tuple(started))
         at, size = 2 * shard_rows, (last_mine.shape[0] - 2 * shard_rows) // 2
         packed = sum(

time: 269 us -> 269 us (level)
    pallas_call x51 -> x52, Pallas kernels: 76 us -> 75.8 us  [call(): *made, Order.token = build(max(counts[-1], 1))(*arrays)]
  transfers between devices with their start and end apart: 54 -> 54, of which waited for: 29 -> 30; matrix products, arithmetic and copies ran while one was open for 1% -> 1% of each run, Pallas kernels for 23% -> 23%
where the time goes in v2:
time: 269 us; the launch traced here: 265 us
  waiting for transfers between devices  124 us (46%)
  Pallas kernels  75.8 us (28%)
  starting transfers between devices  58.4 us (22%)
  local copies, waits for them, and re-layouts  3.91 us (1%)
    ppermute x54, waiting for transfers between devices, permute(): return lax.ppermute(value, AXES, pairs)  124 us
    pallas_call x52, Pallas kernels, call(): *made, Order.token = build(max(counts[-1], 1))(*arrays)  75.8 us
    ppermute x54, starting transfers between devices, permute(): return lax.ppermute(value, AXES, pairs)  58.4 us
  transfers between devices with their start and end apart: 54, of which 30 were waited for; matrix products, arithmetic and copies ran while one was open for 1% of the time, Pallas kernels for 23%

profile of v2, /device:TPU:0, one launch (start us, length us, event | category | flops | bytes accessed | tf_op | source)
XLA Modules:
  0.0 264.6 jit_solution(16810894220382090647)
XLA Ops:
  1.3 3.3 %prepare.1 = (bf16[512,768]{1,0:T(8,128)(2,1)}, bf16[2,96,1536]{2,1,0:T(8,128)(2,1)}, bf16[96,768]{1,0:T(8,128)(2,1)}, bf16[96,768]{1,0:T(8,128)(2,1)}, f32[8,128]{1,0:T(8,128)}) custom-call(bf16[1,1024,768]{2,1,0:T(8,128)(2,1)} %refs_8_.2, bf16[2,96,3072]{2,1,0:T(8,128)(2,1)} %refs_3_.4, bf16[2,384,768]{2,1,0:T(8,128)(2,1)} %refs_1_.7, ...), custom_call_target="tpu_custom_call" | custom-call | flops 10000000000 | bytes 1000 | tf_op jit(solution)/shard_map/prepare/pallas_call | solution.py:242
  14.9 11.1 %collective-permute-done.refs_2_.refs_9_ = bf16[512,768]{1,0:T(8,128)(2,1)S(1)} collective-permute-done((bf16[512,768]{1,0:T(8,128)(2,1)}, bf16[512,768]{1,0:T(8,128)(2,1)S(1)}, u32[]{:S(2)}, u32[]{:S(2)}) %collective-permute-start) | collective-permute-done | bytes 786464 | tf_op jit(solution)/shard_map/ppermute | solution.py:43
  33.9 3.4 %first_mix.1 = (bf16[512,512]{1,0:T(8,128)(2,1)S(1)}, bf16[512,512]{1,0:T(8,128)(2,1)S(1)}, f32[512,768]{1,0:T(8,128)S(1)}, f32[512,1]{1,0:T(8,128)S(1)}, bf16[5...) custom-call(s32[16]{0:T(128)S(1)} %select_n.89.refs_0_, bf16[1,1024,768]{2,1,0:T(8,128)(2,1)S(1)} %copy-done.6, ...), custom_call_target="tpu_custom_call" | custom-call | flops 10000000000 | bytes 1000 | tf_op jit(solution)/shard_map/first_mix/pallas_call | solution.py:242
  40.7 6.0 %collective-permute-done.10.refs_1_ = bf16[2,96,768]{2,1,0:T(8,128)(2,1)S(1)} collective-permute-done((bf16[2,96,768]{2,1,0:T(8,128)(2,1)S(1)}, bf16[2,96,768]{2,1,0:T(8,128)(2,1)S(1)}, u32[]{:S(2)}, u32[]{:S(2)}) %collective-permute-start.10) | collective-permute-done | bytes 294944 | tf_op jit(solution)/shard_map/ppermute | solution.py:43
  49.5 5.8 %expand.2 = (bf16[2,1024,768]{2,1,0:T(8,128)(2,1)S(1)}, bf16[2,1024,768]{2,1,0:T(8,128)(2,1)S(1)}, bf16[2,768,768]{2,1,0:T(8,128)(2,1)S(1)}, f32[8,128]{1,0:T(8,128)S(1)}) custom-call(bf16[512,768]{1,0:T(8,128)(2,1)S(1)} %get-tuple-element.177.refs_0_.refs_3_, bf16[512,768]{1,0:T(8,128)(2,1)S(1)} %collective-permute-done.8.refs_1_.refs_4_, ...), custom_call_target="tpu_custom_call" | custom-call | flops 10000000000 | bytes 1000 | tf_op jit(solution)/shard_map/expand/pallas_call | solution.py:242
  55.4 3.6 %collective-permute-done.11.refs_3_ = bf16[3,96,768]{2,1,0:T(8,128)(2,1)S(1)} collective-permute-done((bf16[3,96,768]{2,1,0:T(8,128)(2,1)S(1)}, bf16[3,96,768]{2,1,0:T(8,128)(2,1)S(1)}, u32[]{:S(2)}, u32[]{:S(2)}) %collective-permute-start.11) | collective-permute-done | bytes 442400 | tf_op jit(solution)/shard_map/ppermute | solution.py:43
  59.6 4.4 %collective-permute-done.14.refs_1_ = bf16[2,192,384]{2,1,0:T(8,128)(2,1)S(1)} collective-permute-done((bf16[2,192,384]{2,1,0:T(8,128)(2,1)S(1)}, bf16[2,192,384]{2,1,0:T(8,128)(2,1)S(1)}, u32[]{:S(2)}, u32[]{:S(2)}) %collective-permute-start.14) | collective-permute-done | bytes 294944 | tf_op jit(solution)/shard_map/ppermute | solution.py:43
  65.4 4.7 %collective-permute-done.13.refs_5_ = bf16[3,96,768]{2,1,0:T(8,128)(2,1)S(1)} collective-permute-done((bf16[3,96,768]{2,1,0:T(8,128)(2,1)S(1)}, bf16[3,96,768]{2,1,0:T(8,128)(2,1)S(1)}, u32[]{:S(2)}, u32[]{:S(2)}) %collective-permute-start.13) | collective-permute-done | bytes 442400 | tf_op jit(solution)/shard_map/ppermute | solution.py:43
  70.1 5.2 %contract.2 = (f32[512,768]{1,0:T(8,128)S(1)}, bf16[512,768]{1,0:T(8,128)(2,1)S(1)}, bf16[1536,768]{1,0:T(8,128)(2,1)S(1)}, f32[8,128]{1,0:T(8,128)S(1)}) custom-call(bf16[2,1024,768]{2,1,0:T(8,128)(2,1)S(1)} %get-tuple-element.181.refs_0_, bf16[2,384,768]{2,1,0:T(8,128)(2,1)S(1)} %copy-done.8, bf16[3,96,768]{2,1,0:T(8,128)(2,1)S(1)} %get-tuple-element.182.refs_2_, ...), custom_call_target="tpu_custom_call" | custom-call | flops 10000000000 | bytes 1000 | tf_op jit(solution)/shard_map/contract/pallas_call | solution.py:242
  82.3 3.1 %middle.1 = (f32[512,768]{1,0:T(8,128)S(1)}, f32[512,1]{1,0:T(8,128)S(1)}, f32[512,768]{1,0:T(8,128)S(1)}, f32[512,1]{1,0:T(8,128)S(1)}, bf16[512,768]{1,0:T(8,128)(2,1)S(1)}, /*index=5*/f32[8,128]{1,0:T(8,128)S(1)}) custom-call(f32[512,768]{1,0:T(8,128)S(1)} %get-tuple-element.189.refs_0_, bf16[512,768]{1,0:T(8,128)(2,1)S(1)} %collective-permute-done.15.refs_1_, ...), custom_call_target="tpu_custom_call" | custom-call | flops 100000000 | bytes 1000 | tf_op jit(solution)/shard_map/middle/pallas_call | solution.py:242
  85.5 9.7 %collective-permute-done.20.refs_8_ = bf16[3,192,384]{2,1,0:T(8,128)(2,1)S(1)} collective-permute-done((bf16[3,192,384]{2,1,0:T(8,128)(2,1)S(1)}, bf16[3,192,384]{2,1,0:T(8,128)(2,1)S(1)}, u32[]{:S(2)}, u32[]{:S(2)}) %collective-permute-start.20) | collective-permute-done | bytes 442400 | tf_op jit(solution)/shard_map/ppermute | solution.py:43
  96.8 5.9 %expand.3 = (bf16[2,1024,768]{2,1,0:T(8,128)(2,1)S(1)}, bf16[2,1024,768]{2,1,0:T(8,128)(2,1)S(1)}, bf16[2,768,768]{2,1,0:T(8,128)(2,1)S(1)}, f32[8,128]{1,0:T(8,128)S(1)}) custom-call(bf16[512,768]{1,0:T(8,128)(2,1)S(1)} %get-tuple-element.200.refs_0_.refs_3_, bf16[512,768]{1,0:T(8,128)(2,1)S(1)} %collective-permute-done.19.refs_1_.refs_4_, ...), custom_call_target="tpu_custom_call" | custom-call | flops 10000000000 | bytes 1000 | tf_op jit(solution)/shard_map/expand/pallas_call | solution.py:242
  103.6 5.2 %contract.3 = (f32[512,768]{1,0:T(8,128)S(1)}, bf16[512,768]{1,0:T(8,128)(2,1)S(1)}, bf16[1536,768]{1,0:T(8,128)(2,1)S(1)}, f32[8,128]{1,0:T(8,128)S(1)}) custom-call(bf16[2,1024,768]{2,1,0:T(8,128)(2,1)S(1)} %get-tuple-element.206.refs_0_, bf16[2,384,768]{2,1,0:T(8,128)(2,1)S(1)} %copy-done.8, bf16[3,96,768]{2,1,0:T(8,128)(2,1)S(1)} %get-tuple-element.204.refs_2_, ...), custom_call_target="tpu_custom_call" | custom-call | flops 10000000000 | bytes 1000 | tf_op jit(solution)/shard_map/contract/pallas_call | solution.py:242
  120.8 8.2 %shrink.2 = (bf16[2,4,192,384]{3,2,1,0:T(8,128)(2,1)S(1)}, bf16[2,4,192,384]{3,2,1,0:T(8,128)(2,1)S(1)}, f32[1,3072]{1,0:T(1,128)S(1)}, f32[512,768]{1,0:T(8,128...) custom-call(bf16[512,768]{1,0:T(8,128)(2,1)S(1)} %get-tuple-element.213.refs_1_.refs_0_, ...), custom_call_target="tpu_custom_call" | custom-call | flops 10000000000 | bytes 1000 | tf_op jit(solution)/shard_map/shrink/pallas_call | solution.py:242
  130.4 5.4 %collective-permute-done.27.refs_1_ = bf16[2,4,96,768]{3,2,1,0:T(8,128)(2,1)S(1)} collective-permute-done((bf16[2,4,96,768]{3,2,1,0:T(8,128)(2,1)S(1)}, bf16[2,4,96,768]{3,2,1,0:T(8,128)(2,1)S(1)}, u32[]{:S(2)}, u32[]{:S(2)}) %collective-permute-start.27) | collective-permute-done | bytes 1179680 | tf_op jit(solution)/shard_map/ppermute | solution.py:43
  135.8 4.0 %relay.1 = (f32[8,768]{1,0:T(8,128)S(1)}, f32[512,768]{1,0:T(8,128)S(1)}, bf16[512,768]{1,0:T(8,128)(2,1)S(1)}, f32[8,768]{1,0:T(8,128)S(1)}, f32[8,128]{1,0:T(8,128)S(1)}) custom-call(f32[512,768]{1,0:T(8,128)S(1)} %get-tuple-element.219.refs_0_, bf16[512,768]{1,0:T(8,128)(2,1)S(1)} %collective-permute-done.26.refs_1_, ...), custom_call_target="tpu_custom_call" | custom-call | flops 10000000000 | bytes 1000 | tf_op jit(solution)/shard_map/relay/pallas_call | solution.py:242
  141.7 11.8 %collective-permute-done.30.refs_1_ = bf16[2,4,192,384]{3,2,1,0:T(8,128)(2,1)S(1)} collective-permute-done((bf16[2,4,192,384]{3,2,1,0:T(8,128)(2,1)S(1)}, bf16[2,4,192,384]{3,2,1,0:T(8,128)(2,1)S(1)}, u32[]{:S(2)}, u32[]{:S(2)}) %collective-permute-start.30) | collective-permute-done | bytes 1179680 | tf_op jit(solution)/shard_map/ppermute | solution.py:43
  155.4 2.9 %grad_out.3 = (bf16[2,4,96,768]{3,2,1,0:T(8,128)(2,1)S(1)}, bf16[2,4,96,768]{3,2,1,0:T(8,128)(2,1)S(1)}, f32[8,128]{1,0:T(8,128)S(1)}) custom-call(bf16[2,1024,768]{2,1,0:T(8,128)(2,1)S(1)} %copy-done.18, bf16[512,768]{1,0:T(8,128)(2,1)S(1)} %get-tuple-element.228.refs_1_.refs_0_, bf16[512,768]{1,0:T(8,128)(2,1)S(1)} %collective-permute-done.28.refs_2_.refs_1_, ...), custom_call_target="tpu_custom_call" | custom-call | flops 10000000000 | bytes 1000 | tf_op jit(solution)/shard_map/grad_out/pallas_call | solution.py:242
  158.5 5.1 %collective-permute-done.31.refs_2_ = bf16[768,384]{1,0:T(8,128)(2,1)S(1)} collective-permute-done((bf16[768,384]{1,0:T(8,128)(2,1)S(1)}, bf16[768,384]{1,0:T(8,128)(2,1)S(1)}, u32[]{:S(2)}, u32[]{:S(2)}) %collective-permute-start.31) | collective-permute-done | bytes 589856 | tf_op jit(solution)/shard_map/ppermute | solution.py:43
  167.0 8.4 %shrink.3 = (bf16[2,4,192,384]{3,2,1,0:T(8,128)(2,1)S(1)}, bf16[2,4,192,384]{3,2,1,0:T(8,128)(2,1)S(1)}, f32[1,3072]{1,0:T(1,128)S(1)}, f32[512,768]{1,0:T(8,128...) custom-call(bf16[512,768]{1,0:T(8,128)(2,1)S(1)} %get-tuple-element.228.refs_1_.refs_0_, ...), custom_call_target="tpu_custom_call" | custom-call | flops 10000000000 | bytes 1000 | tf_op jit(solution)/shard_map/shrink/pallas_call | solution.py:242
  182.1 3.3 %collective-permute-start.38 = (bf16[384,384]{1,0:T(8,128)(2,1)S(1)}, bf16[384,384]{1,0:T(8,128)(2,1)S(1)}, u32[]{:S(2)}, u32[]{:S(2)}) collective-permute-start(bf16[384,384]{1,0:T(8,128)(2,1)S(1)} %get-tuple-element.269), channel_id=1, source_target_pairs={{0,4},{1,5},{2,6},{3,7},{4,0},{5,1},{6,2},{7,3},{8,12},{9,13},{10,... | collective-permute-start | bytes 884744 | tf_op jit(solution)/shard_map/ppermute | solution.py:43
  185.4 3.3 %last.1 = (bf16[512,768]{1,0:T(8,128)(2,1)S(1)}, bf16[512,768]{1,0:T(8,128)(2,1)S(1)}, bf16[64,384]{1,0:T(8,128)(2,1)S(1)}, f32[8,128]{1,0:T(8,128)S(1)}) custom-call(f32[512,768]{1,0:T(8,128)S(1)} %get-tuple-element.243.refs_0_, bf16[512,768]{1,0:T(8,128)(2,1)S(1)} %collective-permute-done.32.refs_1_, f32[512,768]{1,0:T(8,128)S(1)} %get-tuple-element.245.refs_2_, ...), custom_call_target="tpu_custom_call" | custom-call | flops 10000000000 | bytes 1000 | tf_op jit(solution)/shard_map/last/pallas_call | solution.py:242
  188.7 8.8 %collective-permute-done.36.refs_2_ = bf16[384,768]{1,0:T(8,128)(2,1)S(1)} collective-permute-done((bf16[384,768]{1,0:T(8,128)(2,1)S(1)}, bf16[384,768]{1,0:T(8,128)(2,1)S(1)}, u32[]{:S(2)}, u32[]{:S(2)}) %collective-permute-start.36) | collective-permute-done | bytes 589856 | tf_op jit(solution)/shard_map/ppermute | solution.py:43
  197.7 3.5 %collective-permute-done.35.refs_1_ = bf16[2,4,192,384]{3,2,1,0:T(8,128)(2,1)S(1)} collective-permute-done((bf16[2,4,192,384]{3,2,1,0:T(8,128)(2,1)S(1)}, bf16[2,4,192,384]{3,2,1,0:T(8,128)(2,1)S(1)}, u32[]{:S(2)}, u32[]{:S(2)}) %collective-permute-start.35) | collective-permute-done | bytes 1179680 | tf_op jit(solution)/shard_map/ppermute | solution.py:43
  202.2 5.2 %collective-permute-start.43 = (bf16[192,384]{1,0:T(8,128)(2,1)S(1)}, bf16[192,384]{1,0:T(8,128)(2,1)S(1)}, u32[]{:S(2)}, u32[]{:S(2)}) collective-permute-start(bf16[192,384]{1,0:T(8,128)(2,1)S(1)} %get-tuple-element.278), channel_id=1, source_target_pairs={{0,2},{1,3},{2,0},{3,1},{4,6},{5,7},{6,4},{7,5},{8,10},{9,11},{10,... | collective-permute-start | bytes 442376 | tf_op jit(solution)/shard_map/ppermute | solution.py:43
  207.4 4.5 %collective-permute-done.37.refs_2_ = bf16[832,384]{1,0:T(8,128)(2,1)S(1)} collective-permute-done((bf16[832,384]{1,0:T(8,128)(2,1)S(1)}, bf16[832,384]{1,0:T(8,128)(2,1)S(1)}, u32[]{:S(2)}, u32[]{:S(2)}) %collective-permute-start.37) | collective-permute-done | bytes 639008 | tf_op jit(solution)/shard_map/ppermute | solution.py:43
  215.7 12.5 %collective-permute-done.42.refs_3_ = bf16[192,768]{1,0:T(8,128)(2,1)S(1)} collective-permute-done((bf16[192,768]{1,0:T(8,128)(2,1)S(1)}, bf16[192,768]{1,0:T(8,128)(2,1)S(1)}, u32[]{:S(2)}, u32[]{:S(2)}) %collective-permute-start.42) | collective-permute-done | bytes 294944 | tf_op jit(solution)/shard_map/ppermute | solution.py:43
  228.5 3.7 %collective-permute-done.41.refs_3_ = bf16[448,384]{1,0:T(8,128)(2,1)S(1)} collective-permute-done((bf16[448,384]{1,0:T(8,128)(2,1)S(1)}, bf16[448,384]{1,0:T(8,128)(2,1)S(1)}, u32[]{:S(2)}, u32[]{:S(2)}) %collective-permute-start.41) | collective-permute-done | bytes 344096 | tf_op jit(solution)/shard_map/ppermute | solution.py:43
  238.2 2.9 %collective-permute-done.48.refs_2_ = bf16[192,768]{1,0:T(8,128)(2,1)S(1)} collective-permute-done((bf16[192,768]{1,0:T(8,128)(2,1)S(1)}, bf16[192,768]{1,0:T(8,128)(2,1)S(1)}, u32[]{:S(2)}, u32[]{:S(2)}) %collective-permute-start.48) | collective-permute-done | bytes 294944 | tf_op jit(solution)/shard_map/ppermute | solution.py:43
  246.5 4.0 %collective-permute-done.51.refs_3_ = bf16[192,768]{1,0:T(8,128)(2,1)S(1)} collective-permute-done((bf16[192,768]{1,0:T(8,128)(2,1)S(1)}, bf16[192,768]{1,0:T(8,128)(2,1)S(1)}, u32[]{:S(2)}, u32[]{:S(2)}) %collective-permute-start.51) | collective-permute-done | bytes 294944 | tf_op jit(solution)/shard_map/ppermute | solution.py:43
  250.5 3.1 %collective-permute-done.49.refs_1_ = bf16[256,768]{1,0:T(8,128)(2,1)S(1)} collective-permute-done((bf16[256,768]{1,0:T(8,128)(2,1)S(1)}, bf16[256,768]{1,0:T(8,128)(2,1)S(1)}, u32[]{:S(2)}, u32[]{:S(2)}) %collective-permute-start.49) | collective-permute-done | bytes 393248 | tf_op jit(solution)/shard_map/ppermute | solution.py:43
  255.3 3.0 %collect.3 = (f32[2,96,3072]{2,1,0:T(8,128)}, f32[2,384,768]{2,1,0:T(8,128)}, f32[8,128]{1,0:T(8,128)S(1)}) custom-call(bf16[192,768]{1,0:T(8,128)(2,1)S(1)} %get-tuple-element.295.refs_0_, bf16[192,768]{1,0:T(8,128)(2,1)S(1)} %collective-permute-done.50.refs_1_, bf16[192,768]{1,0:T(8,128)(2,1)S(1)} %collective-permute-done.48.refs_2_, ...), custom_call_target="tpu_custom_call" | custom-call | flops 10000000000 | bytes 1000 | tf_op jit(solution)/shard_map/collect/pallas_call | solution.py:242
  (211 shorter events, 87.9 us)
Async XLA Ops:
  5.1 20.9 %collective-permute-start = (bf16[512,768]{1,0:T(8,128)(2,1)}, bf16[512,768]{1,0:T(8,128)(2,1)S(1)}, u32[]{:S(2)}, u32[]{:S(2)}) collective-permute-start(bf16[512,768]{1,0:T(8,128)(2,1)} %get-tuple-element.161), channel_id=1, source_target_pairs={{0,8},{1,9},{2,10},{3,11},{4,12},{5,13},{6,14},{7,15},{8,0},{9,1},... | collective-permute-start | bytes 2359304 | tf_op jit(solution)/shard_map/ppermute | solution.py:43
  9.3 16.7 %collective-permute-start.3 = (bf16[192,384]{1,0:T(8,128)(2,1)S(1)}, bf16[192,384]{1,0:T(8,128)(2,1)S(1)}, u32[]{:S(2)}, u32[]{:S(2)}) collective-permute-start(bf16[192,384]{1,0:T(8,128)(2,1)S(1)} %get-tuple-element.168), channel_id=1, source_target_pairs={{0,2},{1,3},{2,0},{3,1},{4,6},{5,7},{6,4},{7,5},{8,10},{9,11},{10,... | collective-permute-start | bytes 442376 | tf_op jit(solution)/shard_map/ppermute | solution.py:43
  10.9 15.1 %collective-permute-start.4 = (bf16[192,384]{1,0:T(8,128)(2,1)S(1)}, bf16[192,384]{1,0:T(8,128)(2,1)S(1)}, u32[]{:S(2)}, u32[]{:S(2)}) collective-permute-start(bf16[192,384]{1,0:T(8,128)(2,1)S(1)} %get-tuple-element.168), channel_id=1, source_target_pairs={{0,4},{1,5},{2,6},{3,7},{4,0},{5,1},{6,2},{7,3},{8,12},{9,13},{10,... | collective-permute-start | bytes 442376 | tf_op jit(solution)/shard_map/ppermute | solution.py:43
  13.5 12.5 %collective-permute-start.5 = (bf16[192,384]{1,0:T(8,128)(2,1)S(1)}, bf16[192,384]{1,0:T(8,128)(2,1)S(1)}, u32[]{:S(2)}, u32[]{:S(2)}) collective-permute-start(bf16[192,384]{1,0:T(8,128)(2,1)S(1)} %get-tuple-element.168), channel_id=1, source_target_pairs={{0,6},{1,7},{2,4},{3,5},{4,2},{5,3},{6,0},{7,1},{8,14},{9,15},{10,... | collective-permute-start | bytes 442376 | tf_op jit(solution)/shard_map/ppermute | solution.py:43
  14.2 16.9 %collective-permute-start.2 = (bf16[3,96,768]{2,1,0:T(8,128)(2,1)S(1)}, bf16[3,96,768]{2,1,0:T(8,128)(2,1)S(1)}, u32[]{:S(2)}, u32[]{:S(2)}) collective-permute-start(bf16[3,96,768]{2,1,0:T(8,128)(2,1)S(1)} %get-tuple-element.167.refs_0_), channel_id=1, source_target_pairs={{0,2},{1,3},{2,0},{3,1},{4,6},{5,7},{6,4},{7,5},{8,10},{9,11},{10,... | collective-permute-start | bytes 1327112 | tf_op jit(solution)/shard_map/ppermute | solution.py:43
  26.0 12.9 %collective-permute-start.6 = (bf16[3,192,384]{2,1,0:T(8,128)(2,1)S(1)}, bf16[3,192,384]{2,1,0:T(8,128)(2,1)S(1)}, u32[]{:S(2)}, u32[]{:S(2)}) collective-permute-start(bf16[3,192,384]{2,1,0:T(8,128)(2,1)S(1)} %get-tuple-element.175.refs_5_), channel_id=1, source_target_pairs={{0,8},{1,17},{2,10},{3,19},{4,12},{5,21},{6,14},{7,23},{8,0},{9,25... | collective-permute-start | bytes 1327112 | tf_op jit(solution)/shard_map/ppermute | solution.py:43
  27.9 11.1 %collective-permute-start.7 = (bf16[3,192,384]{2,1,0:T(8,128)(2,1)S(1)}, bf16[3,192,384]{2,1,0:T(8,128)(2,1)S(1)}, u32[]{:S(2)}, u32[]{:S(2)}) collective-permute-start(bf16[3,192,384]{2,1,0:T(8,128)(2,1)S(1)} %get-tuple-element.175.refs_5_), channel_id=1, source_target_pairs={{0,16},{1,9},{2,18},{3,11},{4,20},{5,13},{6,22},{7,15},{8,24},{9,1... | collective-permute-start | bytes 1327112 | tf_op jit(solution)/shard_map/ppermute | solution.py:43
  31.1 15.5 %collective-permute-start.10 = (bf16[2,96,768]{2,1,0:T(8,128)(2,1)S(1)}, bf16[2,96,768]{2,1,0:T(8,128)(2,1)S(1)}, u32[]{:S(2)}, u32[]{:S(2)}) collective-permute-start(bf16[2,96,768]{2,1,0:T(8,128)(2,1)S(1)} %get-tuple-element.179.refs_0_), channel_id=1, source_target_pairs={{0,4},{1,5},{2,6},{3,7},{4,0},{5,1},{6,2},{7,3},{8,12},{9,13},{10,... | collective-permute-start | bytes 884744 | tf_op jit(solution)/shard_map/ppermute | solution.py:43
  46.7 12.3 %collective-permute-start.11 = (bf16[3,96,768]{2,1,0:T(8,128)(2,1)S(1)}, bf16[3,96,768]{2,1,0:T(8,128)(2,1)S(1)}, u32[]{:S(2)}, u32[]{:S(2)}) collective-permute-start(bf16[3,96,768]{2,1,0:T(8,128)(2,1)S(1)} %get-tuple-element.182.refs_2_), channel_id=1, source_target_pairs={{0,8},{1,17},{2,10},{3,19},{4,12},{5,21},{6,14},{7,23},{8,0},{9,25... | collective-permute-start | bytes 1327112 | tf_op jit(solution)/shard_map/ppermute | solution.py:43
  49.5 14.5 %collective-permute-start.14 = (bf16[2,192,384]{2,1,0:T(8,128)(2,1)S(1)}, bf16[2,192,384]{2,1,0:T(8,128)(2,1)S(1)}, u32[]{:S(2)}, u32[]{:S(2)}) collective-permute-start(bf16[2,192,384]{2,1,0:T(8,128)(2,1)S(1)} %get-tuple-element.187.refs_0_), channel_id=1, source_target_pairs={{0,4},{1,5},{2,6},{3,7},{4,0},{5,1},{6,2},{7,3},{8,12},{9,13},{10,... | collective-permute-start | bytes 884744 | tf_op jit(solution)/shard_map/ppermute | solution.py:43
  64.0 11.3 %collective-permute-start.17 = (bf16[3,192,384]{2,1,0:T(8,128)(2,1)S(1)}, bf16[3,192,384]{2,1,0:T(8,128)(2,1)S(1)}, u32[]{:S(2)}, u32[]{:S(2)}) collective-permute-start(bf16[3,192,384]{2,1,0:T(8,128)(2,1)S(1)} %get-tuple-element.197.refs_5_), channel_id=1, source_target_pairs={{0,8},{1,17},{2,10},{3,19},{4,12},{5,21},{6,14},{7,23},{8,0},{9,25... | collective-permute-start | bytes 1327112 | tf_op jit(solution)/shard_map/ppermute | solution.py:43
  64.9 12.0 %collective-permute-start.18 = (bf16[3,192,384]{2,1,0:T(8,128)(2,1)S(1)}, bf16[3,192,384]{2,1,0:T(8,128)(2,1)S(1)}, u32[]{:S(2)}, u32[]{:S(2)}) collective-permute-start(bf16[3,192,384]{2,1,0:T(8,128)(2,1)S(1)} %get-tuple-element.197.refs_5_), channel_id=1, source_target_pairs={{0,16},{1,9},{2,18},{3,11},{4,20},{5,13},{6,22},{7,15},{8,24},{9,1... | collective-permute-start | bytes 1327112 | tf_op jit(solution)/shard_map/ppermute | solution.py:43
  65.4 13.5 %collective-permute-start.16 = (bf16[2,96,768]{2,1,0:T(8,128)(2,1)S(1)}, bf16[2,96,768]{2,1,0:T(8,128)(2,1)S(1)}, u32[]{:S(2)}, u32[]{:S(2)}) collective-permute-start(bf16[2,96,768]{2,1,0:T(8,128)(2,1)S(1)} %get-tuple-element.195.refs_0_), channel_id=1, source_target_pairs={{0,4},{1,5},{2,6},{3,7},{4,0},{5,1},{6,2},{7,3},{8,12},{9,13},{10,... | collective-permute-start | bytes 884744 | tf_op jit(solution)/shard_map/ppermute | solution.py:43
  79.0 16.2 %collective-permute-start.21 = (bf16[3,96,768]{2,1,0:T(8,128)(2,1)S(1)}, bf16[3,96,768]{2,1,0:T(8,128)(2,1)S(1)}, u32[]{:S(2)}, u32[]{:S(2)}) collective-permute-start(bf16[3,96,768]{2,1,0:T(8,128)(2,1)S(1)} %get-tuple-element.204.refs_2_), channel_id=1, source_target_pairs={{0,8},{1,17},{2,10},{3,19},{4,12},{5,21},{6,14},{7,23},{8,0},{9,25... | collective-permute-start | bytes 1327112 | tf_op jit(solution)/shard_map/ppermute | solution.py:43
  80.2 15.0 %collective-permute-start.22 = (bf16[3,96,768]{2,1,0:T(8,128)(2,1)S(1)}, bf16[3,96,768]{2,1,0:T(8,128)(2,1)S(1)}, u32[]{:S(2)}, u32[]{:S(2)}) collective-permute-start(bf16[3,96,768]{2,1,0:T(8,128)(2,1)S(1)} %get-tuple-element.204.refs_2_), channel_id=1, source_target_pairs={{0,16},{1,9},{2,18},{3,11},{4,20},{5,13},{6,22},{7,15},{8,24},{9,1... | collective-permute-start | bytes 1327112 | tf_op jit(solution)/shard_map/ppermute | solution.py:43
  81.8 13.4 %collective-permute-start.20 = (bf16[3,192,384]{2,1,0:T(8,128)(2,1)S(1)}, bf16[3,192,384]{2,1,0:T(8,128)(2,1)S(1)}, u32[]{:S(2)}, u32[]{:S(2)}) collective-permute-start(bf16[3,192,384]{2,1,0:T(8,128)(2,1)S(1)} %collective-permute-done.17.refs_6_), channel_id=1, source_target_pairs={{0,16},{1,9},{2,18},{3,11},{4,20},{5,13},{6,22},{7,15},{8,24},{9,1... | collective-permute-start | bytes 1327112 | tf_op jit(solution)/shard_map/ppermute | solution.py:43
  85.4 11.4 %collective-permute-start.19 = (bf16[512,768]{1,0:T(8,128)(2,1)S(1)}, bf16[512,768]{1,0:T(8,128)(2,1)S(1)}, u32[]{:S(2)}, u32[]{:S(2)}) collective-permute-start(bf16[512,768]{1,0:T(8,128)(2,1)S(1)} %get-tuple-element.200.refs_0_.refs_3_), channel_id=1, source_target_pairs={{0,1},{1,0},{2,3},{3,2},{4,5},{5,4},{6,7},{7,6},{8,9},{9,8},{10,11... | collective-permute-start | bytes 2359304 | tf_op jit(solution)/shard_map/ppermute | solution.py:43
  119.5 16.3 %collective-permute-start.27 = (bf16[2,4,96,768]{3,2,1,0:T(8,128)(2,1)S(1)}, bf16[2,4,96,768]{3,2,1,0:T(8,128)(2,1)S(1)}, u32[]{:S(2)}, u32[]{:S(2)}) collective-permute-start(bf16[2,4,96,768]{3,2,1,0:T(8,128)(2,1)S(1)} %get-tuple-element.226), channel_id=1, source_target_pairs={{0,8},{1,17},{2,10},{3,19},{4,12},{5,21},{6,14},{7,23},{8,0},{9,25... | collective-permute-start | bytes 3538952 | tf_op jit(solution)/shard_map/ppermute | solution.py:43
  129.2 24.3 %collective-permute-start.30 = (bf16[2,4,192,384]{3,2,1,0:T(8,128)(2,1)S(1)}, bf16[2,4,192,384]{3,2,1,0:T(8,128)(2,1)S(1)}, u32[]{:S(2)}, u32[]{:S(2)}) collective-permute-start(bf16[2,4,192,384]{3,2,1,0:T(8,128)(2,1)S(1)} %get-tuple-element.236), channel_id=1, source_target_pairs={{0,8},{1,17},{2,10},{3,19},{4,12},{5,21},{6,14},{7,23},{8,0},{9,25... | collective-permute-start | bytes 3538952 | tf_op jit(solution)/shard_map/ppermute | solution.py:43
  139.9 15.4 %collective-permute-start.28 = (bf16[512,768]{1,0:T(8,128)(2,1)S(1)}, bf16[512,768]{1,0:T(8,128)(2,1)S(1)}, u32[]{:S(2)}, u32[]{:S(2)}) collective-permute-start(bf16[512,768]{1,0:T(8,128)(2,1)S(1)} %get-tuple-element.228.refs_1_.refs_0_), channel_id=1, source_target_pairs={{0,1},{1,0},{2,3},{3,2},{4,5},{5,4},{6,7},{7,6},{8,9},{9,8},{10,11... | collective-permute-start | bytes 2359304 | tf_op jit(solution)/shard_map/ppermute | solution.py:43
  140.1 18.3 %collective-permute-start.29 = (bf16[384,768]{1,0:T(8,128)(2,1)S(1)}, bf16[384,768]{1,0:T(8,128)(2,1)S(1)}, u32[]{:S(2)}, u32[]{:S(2)}) collective-permute-start(bf16[384,768]{1,0:T(8,128)(2,1)S(1)} %get-tuple-element.234), channel_id=1, source_target_pairs={{0,16},{1,9},{2,18},{3,11},{4,20},{5,13},{6,22},{7,15},{8,24},{9,1... | collective-permute-start | bytes 1769480 | tf_op jit(solution)/shard_map/ppermute | solution.py:43
  163.7 13.7 %collective-permute-start.34 = (bf16[192,768]{1,0:T(8,128)(2,1)S(1)}, bf16[192,768]{1,0:T(8,128)(2,1)S(1)}, u32[]{:S(2)}, u32[]{:S(2)}) collective-permute-start(bf16[192,768]{1,0:T(8,128)(2,1)S(1)} %get-tuple-element.255), channel_id=1, source_target_pairs={{0,4},{1,5},{2,6},{3,7},{4,0},{5,1},{6,2},{7,3},{8,12},{9,13},{10,... | collective-permute-start | bytes 884744 | tf_op jit(solution)/shard_map/ppermute | solution.py:43
  164.7 16.5 %collective-permute-start.33 = (bf16[2,4,96,768]{3,2,1,0:T(8,128)(2,1)S(1)}, bf16[2,4,96,768]{3,2,1,0:T(8,128)(2,1)S(1)}, u32[]{:S(2)}, u32[]{:S(2)}) collective-permute-start(bf16[2,4,96,768]{3,2,1,0:T(8,128)(2,1)S(1)} %get-tuple-element.254), channel_id=1, source_target_pairs={{0,8},{1,17},{2,10},{3,19},{4,12},{5,21},{6,14},{7,23},{8,0},{9,25... | collective-permute-start | bytes 3538952 | tf_op jit(solution)/shard_map/ppermute | solution.py:43
  175.5 25.7 %collective-permute-start.35 = (bf16[2,4,192,384]{3,2,1,0:T(8,128)(2,1)S(1)}, bf16[2,4,192,384]{3,2,1,0:T(8,128)(2,1)S(1)}, u32[]{:S(2)}, u32[]{:S(2)}) collective-permute-start(bf16[2,4,192,384]{3,2,1,0:T(8,128)(2,1)S(1)} %get-tuple-element.263), channel_id=1, source_target_pairs={{0,8},{1,17},{2,10},{3,19},{4,12},{5,21},{6,14},{7,23},{8,0},{9,25... | collective-permute-start | bytes 3538952 | tf_op jit(solution)/shard_map/ppermute | solution.py:43
  177.5 24.5 %collective-permute-start.39 = (bf16[96,768]{1,0:T(8,128)(2,1)S(1)}, bf16[96,768]{1,0:T(8,128)(2,1)S(1)}, u32[]{:S(2)}, u32[]{:S(2)}) collective-permute-start(bf16[96,768]{1,0:T(8,128)(2,1)S(1)} %get-tuple-element.270), channel_id=1, source_target_pairs={{0,2},{1,3},{2,0},{3,1},{4,6},{5,7},{6,4},{7,5},{8,10},{9,11},{10,... | collective-permute-start | bytes 442376 | tf_op jit(solution)/shard_map/ppermute | solution.py:43
  181.4 16.2 %collective-permute-start.36 = (bf16[384,768]{1,0:T(8,128)(2,1)S(1)}, bf16[384,768]{1,0:T(8,128)(2,1)S(1)}, u32[]{:S(2)}, u32[]{:S(2)}) collective-permute-start(bf16[384,768]{1,0:T(8,128)(2,1)S(1)} %get-tuple-element.265), channel_id=1, source_target_pairs={{0,16},{1,9},{2,18},{3,11},{4,20},{5,13},{6,22},{7,15},{8,24},{9,1... | collective-permute-start | bytes 1769480 | tf_op jit(solution)/shard_map/ppermute | solution.py:43
  182.1 20.0 %collective-permute-start.38 = (bf16[384,384]{1,0:T(8,128)(2,1)S(1)}, bf16[384,384]{1,0:T(8,128)(2,1)S(1)}, u32[]{:S(2)}, u32[]{:S(2)}) collective-permute-start(bf16[384,384]{1,0:T(8,128)(2,1)S(1)} %get-tuple-element.269), channel_id=1, source_target_pairs={{0,4},{1,5},{2,6},{3,7},{4,0},{5,1},{6,2},{7,3},{8,12},{9,13},{10,... | collective-permute-start | bytes 884744 | tf_op jit(solution)/shard_map/ppermute | solution.py:43
  202.2 13.3 %collective-permute-start.43 = (bf16[192,384]{1,0:T(8,128)(2,1)S(1)}, bf16[192,384]{1,0:T(8,128)(2,1)S(1)}, u32[]{:S(2)}, u32[]{:S(2)}) collective-permute-start(bf16[192,384]{1,0:T(8,128)(2,1)S(1)} %get-tuple-element.278), channel_id=1, source_target_pairs={{0,2},{1,3},{2,0},{3,1},{4,6},{5,7},{6,4},{7,5},{8,10},{9,11},{10,... | collective-permute-start | bytes 442376 | tf_op jit(solution)/shard_map/ppermute | solution.py:43
  207.4 20.9 %collective-permute-start.42 = (bf16[192,768]{1,0:T(8,128)(2,1)S(1)}, bf16[192,768]{1,0:T(8,128)(2,1)S(1)}, u32[]{:S(2)}, u32[]{:S(2)}) collective-permute-start(bf16[192,768]{1,0:T(8,128)(2,1)S(1)} %get-tuple-element.277), channel_id=1, source_target_pairs={{0,4},{1,5},{2,6},{3,7},{4,0},{5,1},{6,2},{7,3},{8,12},{9,13},{10,... | collective-permute-start | bytes 884744 | tf_op jit(solution)/shard_map/ppermute | solution.py:43
  212.0 20.2 %collective-permute-start.41 = (bf16[448,384]{1,0:T(8,128)(2,1)S(1)}, bf16[448,384]{1,0:T(8,128)(2,1)S(1)}, u32[]{:S(2)}, u32[]{:S(2)}) collective-permute-start(bf16[448,384]{1,0:T(8,128)(2,1)S(1)} %get-tuple-element.276.refs_4_), channel_id=1, source_target_pairs={{0,4},{1,5},{2,6},{3,7},{4,0},{5,1},{6,2},{7,3},{8,12},{9,13},{10,... | collective-permute-start | bytes 1032200 | tf_op jit(solution)/shard_map/ppermute | solution.py:43
  214.2 18.2 %collective-permute-start.40 = (bf16[512,768]{1,0:T(8,128)(2,1)S(1)}, bf16[512,768]{1,0:T(8,128)(2,1)S(1)}, u32[]{:S(2)}, u32[]{:S(2)}) collective-permute-start(bf16[512,768]{1,0:T(8,128)(2,1)S(1)} %get-tuple-element.275), channel_id=1, source_target_pairs={{0,8},{1,9},{2,10},{3,11},{4,12},{5,13},{6,14},{7,15},{8,0},{9,1},... | collective-permute-start | bytes 2359304 | tf_op jit(solution)/shard_map/ppermute | solution.py:43
  215.6 18.6 %collective-permute-start.46 = (bf16[96,384]{1,0:T(8,128)(2,1)S(1)}, bf16[96,384]{1,0:T(8,128)(2,1)S(1)}, u32[]{:S(2)}, u32[]{:S(2)}) collective-permute-start(bf16[96,384]{1,0:T(8,128)(2,1)S(1)} %get-tuple-element.286), channel_id=1, source_target_pairs={{0,1},{1,0},{2,3},{3,2},{4,5},{5,4},{6,7},{7,6},{8,9},{9,8},{10,11... | collective-permute-start | bytes 221192 | tf_op jit(solution)/shard_map/ppermute | solution.py:43
  (53 other events, 436.2 us)
